TPU v7x, 256 devices: a whole 4x4x8 slice. The times are simulated.
256 devices in a mesh: band: 64 (over x_hi, y, z), pair: 4 (over x_lo, core).
Axes of the slice: x: 4 (x_hi: 2, x_lo: 2; x = x_hi * 2 + x_lo), y: 4, z: 8, core: 2. Of those that a mesh axis runs over, the one named last changes fastest.
Arguments:
- orbitals: float32 [512, 64, 4096], P('band', 'pair'), may hold values from -6 to 6
- pair_table: int32 [8, 2], replicated, may hold values from 0 to 7, as said below
- partner_offset: int32 [1], replicated, may hold values from 1 to 63
Outputs:
- exchange_field: float32 [512, 64, 4096], P('band', 'pair')
- gram: float32 [512, 8], P('band')
Inputs may be any that keep to these rules, and one draw needn't show every extreme that they name: In each column of pair_table every band 0 to 7 appears at least once.
All inputs are finite; a program needn't handle non-finite values.
Results may differ from a plain program's by a relative error of at most 0.0052.
Values may be sent and summed in bfloat16 or wider, within the bound.
No kernel may reach another device: no remote copies, remote signals or barrier semaphores. Data moves between devices by JAX's collectives and lax.ppermute only.
A program may use at most 128 MiB of HBM per device.

v0:
```python
import math

import jax
import jax.numpy as jnp
import ml_dtypes
import numpy as np
from jax import lax
from jax.experimental import pallas as pl
from jax.experimental.pallas import tpu as pltpu
from jax.sharding import PartitionSpec as P

N = 64
BLK = 8
PAIR = 4
SLAB = 16
LANES = 4096
SCREEN = 0.0025
TILES = 8
CHUNK = TILES * 128
XSTEP = 8
SUB = 8
SPOTS = 64
VMEM_LIMIT = 48 * 1024 * 1024

VMEM = pl.BlockSpec(memory_space=pltpu.VMEM)
SMEM = pl.BlockSpec(memory_space=pltpu.SMEM)


def cas_matrix():
    products = np.outer(np.arange(N), np.arange(N)) % N
    angles = 2.0 * math.pi / N * products
    return np.cos(angles) + np.sin(angles)


def halves(matrix):
    high = matrix.astype(ml_dtypes.bfloat16)
    low = (matrix - high.astype(np.float64)).astype(ml_dtypes.bfloat16)
    return high, low


def three(matrix):
    high, low = halves(matrix)
    return np.concatenate([high, high, low], axis=-1)


def tables():
    cas = cas_matrix()
    order = np.array(
        [
            [(q ^ d) * SLAB + h * SUB + r for h in range(2) for d in range(PAIR) for r in range(SUB)]
            for q in range(PAIR)
        ]
    )
    x_forward = np.stack([three(cas[:, order[q]]) for q in range(PAIR)])
    x_back = np.stack([three(cas[order[q], :]) for q in range(PAIR)])
    y_both = three(cas)
    weave = np.zeros((2, 2, N, 2, 2, N))
    for source in range(2):
        for parity in range(2):
            weave[source, parity, :, parity, source, :] = cas
    weave = weave.reshape(4 * N, 4 * N)
    z_forward = np.stack(halves(weave))
    z_back = np.stack(halves(weave.T.copy()))
    squares = 4.0 * np.sin(math.pi * np.arange(N) / N) ** 2
    total = squares[:, None, None] + squares[None, :, None] + squares[None, None, :]
    kernel = 1.0 / (total + SCREEN) / N**3
    kernel = np.concatenate([kernel, kernel], axis=-1).astype(np.float32)
    return x_forward, x_back, y_both, z_forward, z_back, kernel


def arrange(q_ref, orb_ref, spread_ref, *own):
    for t in range(LANES // 128):
        part = orb_ref[:, :, t * 128 : t * 128 + 128]
        for h in range(2):
            rows = part[:, h * SUB : h * SUB + SUB, :].reshape(BLK * SUB, 128)
            spread_ref[t * 2 + h] = rows.astype(jnp.bfloat16)
    for d in range(PAIR):
        base = (q_ref[0] ^ d) * 2
        for i in range(2):
            own[d][i] = orb_ref[base + i].astype(jnp.bfloat16)


def route(table_ref, offset_ref, held_ref, out_ref, wide, give_ref, take_ref):
    for p in range(BLK):
        first = table_ref[p, 0]
        second = table_ref[p, 1]
        give_ref[first] = second
        take_ref[second] = first

    @pl.loop(0, SPOTS, unroll=4)
    def _(j):
        wide[j] = held_ref[j].astype(jnp.float32).reshape(BLK, SUB, 128)

    @pl.loop(0, SPOTS)
    def _(b):
        below = lax.rem(b - offset_ref[0] + SPOTS, SPOTS)
        above = lax.rem(b + offset_ref[0], SPOTS)
        for q in range(PAIR):
            rows = []
            for i in range(2):
                rows.append(wide[below, give_ref[q * 2 + i]])
                rows.append(wide[above, take_ref[q * 2 + i]])
            out_ref[b * PAIR + q] = jnp.concatenate(rows, axis=0).astype(jnp.bfloat16)


def split(value):
    high = value.astype(jnp.bfloat16)
    low = (value - high.astype(jnp.float32)).astype(jnp.bfloat16)
    return high, low


def left_dot(table, value):
    high, low = split(value)
    stacked = jnp.concatenate([high, low, high], axis=0)
    return jnp.dot(table, stacked, preferred_element_type=jnp.float32)


def right_dot(value, table_ref):
    high, low = split(value)
    out = jnp.dot(high, table_ref[0], preferred_element_type=jnp.float32)
    out += jnp.dot(low, table_ref[0], preferred_element_type=jnp.float32)
    out += jnp.dot(high, table_ref[1], preferred_element_type=jnp.float32)
    return out


def solve(q_ref, *refs):
    own, seen = refs[0:4], refs[4]
    xf_ref, xb_ref, y_ref, zf_ref, zb_ref, k_ref = refs[5:11]
    outs, work = refs[11:15], refs[15]
    q = q_ref[0]
    cast = jnp.float32

    def visiting(tile):
        below, above = [], []
        for h in range(2):
            for d in range(PAIR):
                rows = seen[(tile * 2 + h) * PAIR + (q ^ d)].astype(cast)
                below.append(rows[:SUB])
                above.append(rows[SUB:])
        return jnp.concatenate(below, axis=0), jnp.concatenate(above, axis=0)

    @pl.loop(0, LANES // CHUNK)
    def _(c):
        wide = []
        for t in range(TILES):
            tile = c * TILES + t
            at = pl.ds(pl.multiple_of(tile * 128, 128), 128)
            slabs = [own[d][0, :, at].astype(cast) for d in range(PAIR)]
            mine = jnp.concatenate(
                [slabs[d][h * SUB : h * SUB + SUB] for h in range(2) for d in range(PAIR)], axis=0
            )
            below, above = visiting(tile)
            wide += [mine * below, mine * above]
        done_x = left_dot(xf_ref[q], jnp.concatenate(wide, axis=1))
        tall = jnp.concatenate(
            [done_x[:, t * 256 : t * 256 + 256] for t in range(TILES)], axis=0
        )
        done_z = right_dot(tall, zf_ref)
        for t in range(TILES):
            part = done_z[t * N : t * N + N]
            y = (c * TILES + t) * 2
            work[pl.ds(pl.multiple_of(y * N, N), N), :] = part[:, :128]
            work[pl.ds(pl.multiple_of(y * N + N, N), N), :] = part[:, 128:]

    @pl.loop(0, N // XSTEP)
    def _(step):
        spots = [step * XSTEP + i for i in range(XSTEP)]
        value = jnp.concatenate([work[pl.ds(x, N, stride=N), :] for x in spots], axis=1)
        value = left_dot(y_ref[...], value)
        weight = jnp.concatenate([k_ref[x] for x in spots], axis=1)
        value = left_dot(y_ref[...], value * weight)
        for i, x in enumerate(spots):
            work[pl.ds(x, N, stride=N), :] = value[:, i * 128 : i * 128 + 128]

    @pl.loop(0, LANES // CHUNK)
    def _(c):
        parts = []
        for t in range(TILES):
            y = (c * TILES + t) * 2
            even = work[pl.ds(pl.multiple_of(y * N, N), N), :]
            odd = work[pl.ds(pl.multiple_of(y * N + N, N), N), :]
            parts.append(jnp.concatenate([even, odd], axis=1))
        done_z = right_dot(jnp.concatenate(parts, axis=0), zb_ref)
        wide = jnp.concatenate([done_z[t * N : t * N + N] for t in range(TILES)], axis=1)
        pot = left_dot(xb_ref[q], wide)
        for t in range(TILES):
            tile = c * TILES + t
            at = pl.ds(pl.multiple_of(tile * 128, 128), 128)
            below, above = visiting(tile)
            field = pot[:, t * 256 : t * 256 + 128] * below
            field += pot[:, t * 256 + 128 : t * 256 + 256] * above
            for d in range(PAIR):
                rows = [
                    field[(h * PAIR + d) * SUB : (h * PAIR + d + 1) * SUB] for h in range(2)
                ]
                outs[d][:, at] = jnp.concatenate(rows, axis=0).astype(jnp.bfloat16)


def assemble(q_ref, orb_ref, *refs):
    parts, field_ref, gram_ref, flat = refs[0:8], refs[8], refs[9], refs[10]
    for d in range(PAIR):
        base = (q_ref[0] ^ d) * 2
        for i in range(2):
            rows = parts[i * PAIR + d][...]
            field_ref[base + i] = rows.astype(jnp.float32)
            flat[pl.ds(pl.multiple_of((base + i) * SLAB, SLAB), SLAB), :] = rows
    rows = BLK * SLAB
    high, low = split(orb_ref[...].reshape(rows, LANES))
    dims = (((1,), (1,)), ((), ()))
    cross = lax.dot_general(high, flat[...], dims, preferred_element_type=jnp.float32)
    cross += lax.dot_general(low, flat[...], dims, preferred_element_type=jnp.float32)
    down = lax.broadcasted_iota(jnp.int32, (rows, rows), 0)
    along = lax.broadcasted_iota(jnp.int32, (rows, rows), 1)
    cross = jnp.where(down % SLAB == along % SLAB, cross, 0.0)
    summed = jnp.sum(cross.reshape(BLK, SLAB, rows), axis=1)
    pick_at = lax.broadcasted_iota(jnp.int32, (rows, BLK), 0) // SLAB
    pick = (pick_at == lax.broadcasted_iota(jnp.int32, (rows, BLK), 1)).astype(jnp.float32)
    gram_ref[...] = lax.dot_general(
        summed,
        pick,
        (((1,), (0,)), ((), ())),
        precision=lax.Precision.HIGHEST,
        preferred_element_type=jnp.float32,
    ) / math.sqrt(N**3)


PARAMS = pltpu.CompilerParams(vmem_limit_bytes=VMEM_LIMIT)
PIECE = jax.ShapeDtypeStruct((2, SLAB, LANES), jnp.bfloat16)
SENT = jax.ShapeDtypeStruct((SLAB, LANES), jnp.bfloat16)


def on_device(orbitals, pair_table, partner_offset):
    q = lax.axis_index("pair").astype(jnp.int32).reshape(1)

    def across(value, d):
        return lax.ppermute(value, "pair", [(i, i ^ d) for i in range(PAIR)])

    spread, *own = pl.pallas_call(
        arrange,
        out_shape=[jax.ShapeDtypeStruct((SPOTS, BLK * SUB, 128), jnp.bfloat16)] + [PIECE] * 4,
        in_specs=[SMEM, VMEM],
        out_specs=[VMEM] * 5,
        compiler_params=PARAMS,
        name="arrange",
    )(q, orbitals)
    own = [own[0]] + [across(own[d], d) for d in range(1, PAIR)]
    held = lax.all_to_all(spread, "band", 0, 0, tiled=True)
    routed = pl.pallas_call(
        route,
        out_shape=jax.ShapeDtypeStruct((SPOTS * PAIR, 4 * SUB, 128), jnp.bfloat16),
        in_specs=[SMEM, SMEM, VMEM],
        out_specs=VMEM,
        scratch_shapes=[
            pltpu.VMEM((SPOTS, BLK, SUB, 128), jnp.float32),
            pltpu.SMEM((BLK,), jnp.int32),
            pltpu.SMEM((BLK,), jnp.int32),
        ],
        compiler_params=PARAMS,
        name="route",
    )(pair_table, partner_offset, held)
    seen = lax.all_to_all(routed, ("band", "pair"), 0, 0, tiled=True)
    consts = [jnp.asarray(t) for t in tables()]
    back = []
    for a in range(2):
        one = pl.BlockSpec((1, SLAB, LANES), lambda i, a=a: (a, 0, 0))
        rows = pl.BlockSpec((SPOTS * PAIR, 2 * SUB, 128), lambda i, a=a: (0, a, 0))
        sent = pl.pallas_call(
            solve,
            grid=(1,),
            out_shape=[SENT] * 4,
            in_specs=[SMEM] + [one] * 4 + [rows] + [VMEM] * 6,
            out_specs=[VMEM] * 4,
            scratch_shapes=[pltpu.VMEM((N * N, 128), jnp.float32)],
            compiler_params=PARAMS,
            cost_estimate=pl.CostEstimate(
                flops=10_000_000_000, bytes_accessed=8_000_000, transcendentals=0
            ),
            name="solve",
        )(q, *own, seen, *consts)
        back += [sent[0]] + [across(sent[d], d) for d in range(1, PAIR)]
    field, gram = pl.pallas_call(
        assemble,
        out_shape=[
            jax.ShapeDtypeStruct((BLK, SLAB, LANES), jnp.float32),
            jax.ShapeDtypeStruct((BLK, BLK), jnp.float32),
        ],
        in_specs=[SMEM] + [VMEM] * 9,
        out_specs=[VMEM] * 2,
        scratch_shapes=[pltpu.VMEM((BLK * SLAB, LANES), jnp.bfloat16)],
        compiler_params=PARAMS,
        name="assemble",
    )(q, orbitals, *back)
    return field, (gram + across(gram, 1)) + (across(gram, 2) + across(gram, 3))


def solution(mesh):
    return jax.shard_map(
        on_device,
        mesh=mesh,
        in_specs=(P("band", "pair", None), P(), P()),
        out_specs=(P("band", "pair", None), P("band", None)),
        check_vma=False,
    )
```

profile of v0, /device:TPU:1, one launch (start us, length us, event | category | flops | bytes accessed | tf_op | source)
XLA Modules:
  0.0 153.7 jit_solution(15263046680368654594)
XLA Ops:
  0.6 0.0 copy-start
  0.6 1.6 %copy-done = f32[8,16,4096]{2,1,0:T(8,128)S(1)} copy-done((f32[8,16,4096]{2,1,0:T(8,128)S(1)}, f32[8,16,4096]{2,1,0:T(8,128)}, u32[]{:S(2)}) %copy-start) | copy-done | bytes 2097176
  2.2 1.3 arrange.1
  3.5 15.1 %all-to-all-start = ((bf16[64,64,128]{2,1,0:T(8,128)(2,1)}), bf16[64,64,128]{2,1,0:T(8,128)(2,1)S(1)}, u32[]{:S(2)}, u32[]{:S(2)}) async-start(bf16[64,64,128]{2,1,0:T(8,128)(2,1)} %get-tuple-element.21), calls=%async_computation | async-start | bytes 2097152 | tf_op jit(solution)/shard_map/all_to_all | solution.py:247
  19.3 0.1 copy.11.table_ref
  19.4 27.3 %all-to-all-done.held_ref = bf16[64,64,128]{2,1,0:T(8,128)(2,1)S(1)} async-done(((bf16[64,64,128]{2,1,0:T(8,128)(2,1)}), bf16[64,64,128]{2,1,0:T(8,128)(2,1)S(1)}, u32[]{:S(2)}, u32[]{:S(2)}) %all-to-all-start) | async-done | bytes 1048608 | tf_op jit(solution)/shard_map/all_to_all | solution.py:247
  46.7 3.9 %route.1 = bf16[256,32,128]{2,1,0:T(8,128)(2,1)} custom-call(s32[8,2]{1,0:T(8,128)S(1)} %copy.11.table_ref, s32[1]{0:T(128)S(6)} %copy.12.offset_ref, bf16[64,64,128]{2,1,0:T(8,128)(2,1)S(1)} %all-to-all-done.held_ref), custom_call_target="tpu_custom_call" | custom-call | tf_op jit(solution)/shard_map/route/pallas_call | solution.py:248
  50.6 9.0 %all-to-all-start.1 = ((bf16[256,32,128]{2,1,0:T(8,128)(2,1)}), bf16[256,32,128]{2,1,0:T(8,128)(2,1)S(1)}, u32[]{:S(2)}, u32[]{:S(2)}) async-start(bf16[256,32,128]{2,1,0:T(8,128)(2,1)} %route.1), calls=%async_computation.1 | async-start | bytes 4194304 | tf_op jit(solution)/shard_map/all_to_all | solution.py:261
  59.6 2.2 %collective-permute-start = (bf16[2,16,4096]{2,1,0:T(8,128)(2,1)}, bf16[2,16,4096]{2,1,0:T(8,128)(2,1)S(1)}, u32[]{:S(2)}, u32[]{:S(2)}) collective-permute-start(bf16[2,16,4096]{2,1,0:T(8,128)(2,1)} %get-tuple-element.18), channel_id=1, source_target_pairs={{0,1},{1,0},{2,3},{3,2},{4,5},{5,4},{6,7},{7,6},{8,9},{9,8},{10,11... | collective-permute-start | bytes 786440 | tf_op jit(solution)/shard_map/ppermute | solution.py:236
  61.8 1.7 %collective-permute-start.2 = (bf16[2,16,4096]{2,1,0:T(8,128)(2,1)S(1)}, bf16[2,16,4096]{2,1,0:T(8,128)(2,1)S(1)}, u32[]{:S(2)}, u32[]{:S(2)}) collective-permute-start(bf16[2,16,4096]{2,1,0:T(8,128)(2,1)S(1)} %get-tuple-element.20), channel_id=1, source_target_pairs={{0,3},{1,2},{2,1},{3,0},{4,7},{5,6},{6,5},{7,4},{8,11},{9,10},{10,... | collective-permute-start | bytes 786440 | tf_op jit(solution)/shard_map/ppermute | solution.py:236
  63.6 11.0 %collective-permute-done.1.refs_2_ = bf16[2,16,4096]{2,1,0:T(8,128)(2,1)S(1)} collective-permute-done((bf16[2,16,4096]{2,1,0:T(8,128)(2,1)}, bf16[2,16,4096]{2,1,0:T(8,128)(2,1)S(1)}, u32[]{:S(2)}, u32[]{:S(2)}) %collective-permute-start.1) | collective-permute-done | bytes 262176 | tf_op jit(solution)/shard_map/ppermute | solution.py:236
  74.5 10.3 %collective-permute-done.2.refs_3_ = bf16[2,16,4096]{2,1,0:T(8,128)(2,1)S(1)} collective-permute-done((bf16[2,16,4096]{2,1,0:T(8,128)(2,1)S(1)}, bf16[2,16,4096]{2,1,0:T(8,128)(2,1)S(1)}, u32[]{:S(2)}, u32[]{:S(2)}) %collective-permute-start.2) | collective-permute-done | bytes 262176 | tf_op jit(solution)/shard_map/ppermute | solution.py:236
  84.8 26.8 %all-to-all-done.1.refs_4_ = bf16[256,32,128]{2,1,0:T(8,128)(2,1)S(1)} async-done(((bf16[256,32,128]{2,1,0:T(8,128)(2,1)}), bf16[256,32,128]{2,1,0:T(8,128)(2,1)S(1)}, u32[]{:S(2)}, u32[]{:S(2)}) %all-to-all-start.1) | async-done | bytes 2097184 | tf_op jit(solution)/shard_map/all_to_all | solution.py:261
  111.7 0.9 copy-done.2
  112.6 0.9 copy-done.4
  113.5 0.8 copy-done.5
  114.3 11.5 %solve.3 = (bf16[16,4096]{1,0:T(8,128)(2,1)S(1)}, bf16[16,4096]{1,0:T(8,128)(2,1)S(1)}, bf16[16,4096]{1,0:T(8,128)(2,1)S(1)}, bf16[16,4096]{1,0:T(8,128)(2,1)S(1)}) custom-call(s32[1]{0:T(128)} %bitcast.q_ref, bf16[2,16,4096]{2,1,0:T(8,128)(2,1)S(1)} %get-tuple-element.17.refs_0_, bf16[2,16,4096]{2,1,0:T(8,128)(2,1)S(1)} %collective-permute-done.refs_1_, ...), custom_call_target="tpu_custom_call" | custom-call | flops 10000000000 | bytes 8000000 | tf_op jit(solution)/shard_map/solve/pallas_call | solution.py:267
  125.8 0.7 collective-permute-start.6
  126.5 0.5 collective-permute-start.7
  127.0 1.2 collective-permute-start.8
  128.2 11.5 %solve.2 = (bf16[16,4096]{1,0:T(8,128)(2,1)S(1)}, bf16[16,4096]{1,0:T(8,128)(2,1)S(1)}, bf16[16,4096]{1,0:T(8,128)(2,1)S(1)}, bf16[16,4096]{1,0:T(8,128)(2,1)S(1)}) custom-call(s32[1]{0:T(128)} %bitcast.q_ref, bf16[2,16,4096]{2,1,0:T(8,128)(2,1)S(1)} %get-tuple-element.17.refs_0_, bf16[2,16,4096]{2,1,0:T(8,128)(2,1)S(1)} %collective-permute-done.refs_1_, ...), custom_call_target="tpu_custom_call" | custom-call | flops 10000000000 | bytes 8000000 | tf_op jit(solution)/shard_map/solve/pallas_call | solution.py:267
  139.7 0.2 collective-permute-start.3
  140.0 0.5 collective-permute-start.4
  140.5 1.5 collective-permute-start.5
  142.0 2.7 %collective-permute-done.4.refs_2_ = bf16[16,4096]{1,0:T(8,128)(2,1)S(1)} collective-permute-done((bf16[16,4096]{1,0:T(8,128)(2,1)S(1)}, bf16[16,4096]{1,0:T(8,128)(2,1)S(1)}, u32[]{:S(2)}, u32[]{:S(2)}) %collective-permute-start.4) | collective-permute-done | bytes 131104 | tf_op jit(solution)/shard_map/ppermute | solution.py:236
  144.7 3.3 %collective-permute-done.5.refs_3_ = bf16[16,4096]{1,0:T(8,128)(2,1)S(1)} collective-permute-done((bf16[16,4096]{1,0:T(8,128)(2,1)S(1)}, bf16[16,4096]{1,0:T(8,128)(2,1)S(1)}, u32[]{:S(2)}, u32[]{:S(2)}) %collective-permute-start.5) | collective-permute-done | bytes 131104 | tf_op jit(solution)/shard_map/ppermute | solution.py:236
  148.0 2.1 %assemble.1 = (f32[8,16,4096]{2,1,0:T(8,128)}, f32[8,8]{1,0:T(8,128)S(1)}) custom-call(s32[1]{0:T(128)} %bitcast.q_ref, f32[8,16,4096]{2,1,0:T(8,128)S(1)} %copy-done.1, bf16[16,4096]{1,0:T(8,128)(2,1)S(1)} %get-tuple-element.22.refs_0_, bf16[16,4096]{1,0:T(8,128)(2,1)S(1)} %collective-permute-done.3.refs_1_, ...), custom_call_target="tpu_custom_call" | custom-call | tf_op jit(solution)/shard_map/assemble/pallas_call | solution.py:281
  150.1 0.3 collective-permute-start.11
  150.4 0.9 collective-permute-start.10
  151.3 0.9 collective-permute-start.9
  152.2 0.9 collective-permute-done.11
  153.1 0.6 add_add_fusion
  (17 shorter events, 0.0 us)
Async XLA Ops:
  0.6 1.6 %copy-start = (f32[8,16,4096]{2,1,0:T(8,128)S(1)}, f32[8,16,4096]{2,1,0:T(8,128)}, u32[]{:S(2)}) copy-start(f32[8,16,4096]{2,1,0:T(8,128)} %orb_ref.3) | copy-start | bytes 6291460
  2.2 17.1 %copy-start.6 = (s32[8,2]{0,1:T(2,128)S(1)}, s32[8,2]{0,1:T(2,128)}, u32[]{:S(2)}) copy-start(s32[8,2]{0,1:T(2,128)} %param.10) | copy-start | bytes 196
  3.5 43.2 %all-to-all-start = ((bf16[64,64,128]{2,1,0:T(8,128)(2,1)}), bf16[64,64,128]{2,1,0:T(8,128)(2,1)S(1)}, u32[]{:S(2)}, u32[]{:S(2)}) async-start(bf16[64,64,128]{2,1,0:T(8,128)(2,1)} %get-tuple-element.21), calls=%async_computation | async-start | bytes 2097152 | tf_op jit(solution)/shard_map/all_to_all | solution.py:247
  50.6 61.0 %copy-start.3 = (bf16[4,64,192]{2,1,0:T(8,128)(2,1)S(1)}, bf16[4,64,192]{2,1,0:T(8,128)(2,1)}, u32[]{:S(2)}) copy-start(bf16[4,64,192]{2,1,0:T(8,128)(2,1)} %constant.15.clone.refs_6_) | copy-start | bytes 294916
  50.6 61.0 %all-to-all-start.1 = ((bf16[256,32,128]{2,1,0:T(8,128)(2,1)}), bf16[256,32,128]{2,1,0:T(8,128)(2,1)S(1)}, u32[]{:S(2)}, u32[]{:S(2)}) async-start(bf16[256,32,128]{2,1,0:T(8,128)(2,1)} %route.1), calls=%async_computation.1 | async-start | bytes 4194304 | tf_op jit(solution)/shard_map/all_to_all | solution.py:261
  59.6 4.0 %collective-permute-start = (bf16[2,16,4096]{2,1,0:T(8,128)(2,1)}, bf16[2,16,4096]{2,1,0:T(8,128)(2,1)S(1)}, u32[]{:S(2)}, u32[]{:S(2)}) collective-permute-start(bf16[2,16,4096]{2,1,0:T(8,128)(2,1)} %get-tuple-element.18), channel_id=1, source_target_pairs={{0,1},{1,0},{2,3},{3,2},{4,5},{5,4},{6,7},{7,6},{8,9},{9,8},{10,11... | collective-permute-start | bytes 786440 | tf_op jit(solution)/shard_map/ppermute | solution.py:236
  61.8 12.7 %collective-permute-start.1 = (bf16[2,16,4096]{2,1,0:T(8,128)(2,1)}, bf16[2,16,4096]{2,1,0:T(8,128)(2,1)S(1)}, u32[]{:S(2)}, u32[]{:S(2)}) collective-permute-start(bf16[2,16,4096]{2,1,0:T(8,128)(2,1)} %get-tuple-element.19), channel_id=1, source_target_pairs={{0,2},{1,3},{2,0},{3,1},{4,6},{5,7},{6,4},{7,5},{8,10},{9,11},{10,... | collective-permute-start | bytes 786440 | tf_op jit(solution)/shard_map/ppermute | solution.py:236
  61.8 23.0 %collective-permute-start.2 = (bf16[2,16,4096]{2,1,0:T(8,128)(2,1)S(1)}, bf16[2,16,4096]{2,1,0:T(8,128)(2,1)S(1)}, u32[]{:S(2)}, u32[]{:S(2)}) collective-permute-start(bf16[2,16,4096]{2,1,0:T(8,128)(2,1)S(1)} %get-tuple-element.20), channel_id=1, source_target_pairs={{0,3},{1,2},{2,1},{3,0},{4,7},{5,6},{6,5},{7,4},{8,11},{9,10},{10,... | collective-permute-start | bytes 786440 | tf_op jit(solution)/shard_map/ppermute | solution.py:236
  111.7 1.0 copy-start.2
  112.6 0.9 copy-start.4
  113.5 0.8 copy-start.5
  125.8 14.7 %collective-permute-start.6 = (bf16[16,4096]{1,0:T(8,128)(2,1)S(1)}, bf16[16,4096]{1,0:T(8,128)(2,1)S(1)}, u32[]{:S(2)}, u32[]{:S(2)}) collective-permute-start(bf16[16,4096]{1,0:T(8,128)(2,1)S(1)} %get-tuple-element.27), channel_id=1, source_target_pairs={{0,1},{1,0},{2,3},{3,2},{4,5},{5,4},{6,7},{7,6},{8,9},{9,8},{10,11... | collective-permute-start | bytes 393224 | tf_op jit(solution)/shard_map/ppermute | solution.py:236
  126.5 15.5 %collective-permute-start.7 = (bf16[16,4096]{1,0:T(8,128)(2,1)S(1)}, bf16[16,4096]{1,0:T(8,128)(2,1)S(1)}, u32[]{:S(2)}, u32[]{:S(2)}) collective-permute-start(bf16[16,4096]{1,0:T(8,128)(2,1)S(1)} %get-tuple-element.28), channel_id=1, source_target_pairs={{0,2},{1,3},{2,0},{3,1},{4,6},{5,7},{6,4},{7,5},{8,10},{9,11},{10,... | collective-permute-start | bytes 393224 | tf_op jit(solution)/shard_map/ppermute | solution.py:236
  127.0 21.0 %copy-start.1 = (f32[8,16,4096]{2,1,0:T(8,128)S(1)}, f32[8,16,4096]{2,1,0:T(8,128)}, u32[]{:S(2)}) copy-start(f32[8,16,4096]{2,1,0:T(8,128)} %orb_ref.3) | copy-start | bytes 6291460
  127.0 15.0 %collective-permute-start.8 = (bf16[16,4096]{1,0:T(8,128)(2,1)S(1)}, bf16[16,4096]{1,0:T(8,128)(2,1)S(1)}, u32[]{:S(2)}, u32[]{:S(2)}) collective-permute-start(bf16[16,4096]{1,0:T(8,128)(2,1)S(1)} %get-tuple-element.29), channel_id=1, source_target_pairs={{0,3},{1,2},{2,1},{3,0},{4,7},{5,6},{6,5},{7,4},{8,11},{9,10},{10,... | collective-permute-start | bytes 393224 | tf_op jit(solution)/shard_map/ppermute | solution.py:236
  139.7 2.2 %collective-permute-start.3 = (bf16[16,4096]{1,0:T(8,128)(2,1)S(1)}, bf16[16,4096]{1,0:T(8,128)(2,1)S(1)}, u32[]{:S(2)}, u32[]{:S(2)}) collective-permute-start(bf16[16,4096]{1,0:T(8,128)(2,1)S(1)} %get-tuple-element.23), channel_id=1, source_target_pairs={{0,1},{1,0},{2,3},{3,2},{4,5},{5,4},{6,7},{7,6},{8,9},{9,8},{10,11... | collective-permute-start | bytes 393224 | tf_op jit(solution)/shard_map/ppermute | solution.py:236
  140.0 4.7 %collective-permute-start.4 = (bf16[16,4096]{1,0:T(8,128)(2,1)S(1)}, bf16[16,4096]{1,0:T(8,128)(2,1)S(1)}, u32[]{:S(2)}, u32[]{:S(2)}) collective-permute-start(bf16[16,4096]{1,0:T(8,128)(2,1)S(1)} %get-tuple-element.24), channel_id=1, source_target_pairs={{0,2},{1,3},{2,0},{3,1},{4,6},{5,7},{6,4},{7,5},{8,10},{9,11},{10,... | collective-permute-start | bytes 393224 | tf_op jit(solution)/shard_map/ppermute | solution.py:236
  140.5 7.5 %collective-permute-start.5 = (bf16[16,4096]{1,0:T(8,128)(2,1)S(1)}, bf16[16,4096]{1,0:T(8,128)(2,1)S(1)}, u32[]{:S(2)}, u32[]{:S(2)}) collective-permute-start(bf16[16,4096]{1,0:T(8,128)(2,1)S(1)} %get-tuple-element.25), channel_id=1, source_target_pairs={{0,3},{1,2},{2,1},{3,0},{4,7},{5,6},{6,5},{7,4},{8,11},{9,10},{10,... | collective-permute-start | bytes 393224 | tf_op jit(solution)/shard_map/ppermute | solution.py:236
  150.1 3.0 %collective-permute-start.11 = (f32[8,8]{1,0:T(8,128)S(1)}, f32[8,8]{1,0:T(8,128)S(1)}, u32[]{:S(2)}, u32[]{:S(2)}) collective-permute-start(f32[8,8]{1,0:T(8,128)S(1)} %get-tuple-element.31), channel_id=1, source_target_pairs={{0,3},{1,2},{2,1},{3,0},{4,7},{5,6},{6,5},{7,4},{8,11},{9,10},{10,... | collective-permute-start | bytes 776 | tf_op jit(solution)/shard_map/ppermute | solution.py:236
  150.4 2.7 %collective-permute-start.10 = (f32[8,8]{1,0:T(8,128)S(1)}, f32[8,8]{1,0:T(8,128)S(1)}, u32[]{:S(2)}, u32[]{:S(2)}) collective-permute-start(f32[8,8]{1,0:T(8,128)S(1)} %get-tuple-element.31), channel_id=1, source_target_pairs={{0,2},{1,3},{2,0},{3,1},{4,6},{5,7},{6,4},{7,5},{8,10},{9,11},{10,... | collective-permute-start | bytes 776 | tf_op jit(solution)/shard_map/ppermute | solution.py:236
  151.3 1.8 %collective-permute-start.9 = (f32[8,8]{1,0:T(8,128)S(1)}, f32[8,8]{1,0:T(8,128)S(1)}, u32[]{:S(2)}, u32[]{:S(2)}) collective-permute-start(f32[8,8]{1,0:T(8,128)S(1)} %get-tuple-element.31), channel_id=1, source_target_pairs={{0,1},{1,0},{2,3},{3,2},{4,5},{5,4},{6,7},{7,6},{8,9},{9,8},{10,11... | collective-permute-start | bytes 776 | tf_op jit(solution)/shard_map/ppermute | solution.py:236
where the time goes:
time: 154 us
  waiting for transfers between devices  82.3 us (53%)
  starting transfers between devices  34.9 us (23%)
  Pallas kernels  30.3 us (20%)
  local copies, waits for them, and re-layouts  4.29 us (3%)
    ppermute x12, waiting for transfers between devices, across(): return lax.ppermute(value, 'pair', [(i, i ^ d) for i in range(PAIR)])  28.2 us
    all_to_all x1, waiting for transfers between devices, on_device(): held = lax.all_to_all(spread, 'band', 0, 0, tiled=True)  27.3 us
    all_to_all x1, waiting for transfers between devices, on_device(): seen = lax.all_to_all(routed, ('band', 'pair'), 0, 0, tiled=True)  26.8 us
    pallas_call x2, Pallas kernels, on_device(): pl.pallas_call(solve, grid=(1,), out_shape=[SENT] * 4, in_specs=[SMEM] +...  23 us
    all_to_all x1, starting transfers between devices, on_device(): held = lax.all_to_all(spread, 'band', 0, 0, tiled=True)  15.1 us
    ppermute x12, starting transfers between devices, across(): return lax.ppermute(value, 'pair', [(i, i ^ d) for i in range(PAIR)])  10.8 us
    all_to_all x1, starting transfers between devices, on_device(): seen = lax.all_to_all(routed, ('band', 'pair'), 0, 0, tiled=True)  8.97 us
    unnamed x15, local copies, waits for them, and re-layouts  4.29 us
  transfers between devices with their start and end apart: 14, of which 7 were waited for; matrix products, arithmetic and copies ran while one was open for 0% of the time, Pallas kernels for 7%

commit v1 on v0

--- a/solution.py
+++ b/solution.py
@@ -15,9 +15,10 @@
 SLAB = 16
 LANES = 4096
 SCREEN = 0.0025
-TILES = 8
+TILES = 32
 CHUNK = TILES * 128
-XSTEP = 8
+XSTEP = 32
+PITCH = 72
 SUB = 8
 SPOTS = 64
 VMEM_LIMIT = 48 * 1024 * 1024
@@ -159,26 +160,26 @@
         for t in range(TILES):
             part = done_z[t * N : t * N + N]
             y = (c * TILES + t) * 2
-            work[pl.ds(pl.multiple_of(y * N, N), N), :] = part[:, :128]
-            work[pl.ds(pl.multiple_of(y * N + N, N), N), :] = part[:, 128:]
+            work[pl.ds(pl.multiple_of(y * PITCH, 8), N), :] = part[:, :128]
+            work[pl.ds(pl.multiple_of(y * PITCH + PITCH, 8), N), :] = part[:, 128:]
 
     @pl.loop(0, N // XSTEP)
     def _(step):
         spots = [step * XSTEP + i for i in range(XSTEP)]
-        value = jnp.concatenate([work[pl.ds(x, N, stride=N), :] for x in spots], axis=1)
+        value = jnp.concatenate([work[pl.ds(x, N, stride=PITCH), :] for x in spots], axis=1)
         value = left_dot(y_ref[...], value)
         weight = jnp.concatenate([k_ref[x] for x in spots], axis=1)
         value = left_dot(y_ref[...], value * weight)
         for i, x in enumerate(spots):
-            work[pl.ds(x, N, stride=N), :] = value[:, i * 128 : i * 128 + 128]
+            work[pl.ds(x, N, stride=PITCH), :] = value[:, i * 128 : i * 128 + 128]
 
     @pl.loop(0, LANES // CHUNK)
     def _(c):
         parts = []
         for t in range(TILES):
             y = (c * TILES + t) * 2
-            even = work[pl.ds(pl.multiple_of(y * N, N), N), :]
-            odd = work[pl.ds(pl.multiple_of(y * N + N, N), N), :]
+            even = work[pl.ds(pl.multiple_of(y * PITCH, 8), N), :]
+            odd = work[pl.ds(pl.multiple_of(y * PITCH + PITCH, 8), N), :]
             parts.append(jnp.concatenate([even, odd], axis=1))
         done_z = right_dot(jnp.concatenate(parts, axis=0), zb_ref)
         wide = jnp.concatenate([done_z[t * N : t * N + N] for t in range(TILES)], axis=1)
@@ -270,7 +271,7 @@
             out_shape=[SENT] * 4,
             in_specs=[SMEM] + [one] * 4 + [rows] + [VMEM] * 6,
             out_specs=[VMEM] * 4,
-            scratch_shapes=[pltpu.VMEM((N * N, 128), jnp.float32)],
+            scratch_shapes=[pltpu.VMEM((N * PITCH, 128), jnp.float32)],
             compiler_params=PARAMS,
             cost_estimate=pl.CostEstimate(
                 flops=10_000_000_000, bytes_accessed=8_000_000, transcendentals=0

time: 154 us -> 144 us (0.935)
  Pallas kernels: 30.3 us -> 20.5 us
    pallas_call x2, Pallas kernels: 23 us -> 13.2 us  [on_device(): pl.pallas_call(solve, grid=(1,), out_shape=[SENT] * 4, in_specs=[SMEM] +...]
  transfers between devices with their start and end apart: 14 -> 14, of which waited for: 7 -> 7; matrix products, arithmetic and copies ran while one was open for 0% -> 0% of each run, Pallas kernels for 7% -> 5%
where the time goes in v1:
time: 144 us
  waiting for transfers between devices  82.3 us (57%)
  starting transfers between devices  34.9 us (24%)
  Pallas kernels  20.5 us (14%)
  local copies, waits for them, and re-layouts  4.29 us (3%)
    ppermute x12, waiting for transfers between devices, across(): return lax.ppermute(value, 'pair', [(i, i ^ d) for i in range(PAIR)])  28.2 us
    all_to_all x1, waiting for transfers between devices, on_device(): held = lax.all_to_all(spread, 'band', 0, 0, tiled=True)  27.3 us
    all_to_all x1, waiting for transfers between devices, on_device(): seen = lax.all_to_all(routed, ('band', 'pair'), 0, 0, tiled=True)  26.8 us
    all_to_all x1, starting transfers between devices, on_device(): held = lax.all_to_all(spread, 'band', 0, 0, tiled=True)  15.1 us
    pallas_call x2, Pallas kernels, on_device(): pl.pallas_call(solve, grid=(1,), out_shape=[SENT] * 4, in_specs=[SMEM] +...  13.2 us
    ppermute x12, starting transfers between devices, across(): return lax.ppermute(value, 'pair', [(i, i ^ d) for i in range(PAIR)])  10.8 us
    all_to_all x1, starting transfers between devices, on_device(): seen = lax.all_to_all(routed, ('band', 'pair'), 0, 0, tiled=True)  8.97 us
    unnamed x15, local copies, waits for them, and re-layouts  4.29 us
  transfers between devices with their start and end apart: 14, of which 7 were waited for; matrix products, arithmetic and copies ran while one was open for 0% of the time, Pallas kernels for 5%

profile of v1, /device:TPU:1, one launch (start us, length us, event | category | flops | bytes accessed | tf_op | source)
XLA Modules:
  0.0 143.9 jit_solution(3604857276072346162)
XLA Ops:
  0.6 0.0 copy-start
  0.6 1.6 %copy-done = f32[8,16,4096]{2,1,0:T(8,128)S(1)} copy-done((f32[8,16,4096]{2,1,0:T(8,128)S(1)}, f32[8,16,4096]{2,1,0:T(8,128)}, u32[]{:S(2)}) %copy-start) | copy-done | bytes 2097176
  2.2 1.3 arrange.1
  3.5 15.1 %all-to-all-start = ((bf16[64,64,128]{2,1,0:T(8,128)(2,1)}), bf16[64,64,128]{2,1,0:T(8,128)(2,1)S(1)}, u32[]{:S(2)}, u32[]{:S(2)}) async-start(bf16[64,64,128]{2,1,0:T(8,128)(2,1)} %get-tuple-element.21), calls=%async_computation | async-start | bytes 2097152 | tf_op jit(solution)/shard_map/all_to_all | solution.py:248
  19.3 0.1 copy.11.table_ref
  19.4 27.3 %all-to-all-done.held_ref = bf16[64,64,128]{2,1,0:T(8,128)(2,1)S(1)} async-done(((bf16[64,64,128]{2,1,0:T(8,128)(2,1)}), bf16[64,64,128]{2,1,0:T(8,128)(2,1)S(1)}, u32[]{:S(2)}, u32[]{:S(2)}) %all-to-all-start) | async-done | bytes 1048608 | tf_op jit(solution)/shard_map/all_to_all | solution.py:248
  46.7 3.9 %route.1 = bf16[256,32,128]{2,1,0:T(8,128)(2,1)} custom-call(s32[8,2]{1,0:T(8,128)S(1)} %copy.11.table_ref, s32[1]{0:T(128)S(6)} %copy.12.offset_ref, bf16[64,64,128]{2,1,0:T(8,128)(2,1)S(1)} %all-to-all-done.held_ref), custom_call_target="tpu_custom_call" | custom-call | tf_op jit(solution)/shard_map/route/pallas_call | solution.py:249
  50.6 9.0 %all-to-all-start.1 = ((bf16[256,32,128]{2,1,0:T(8,128)(2,1)}), bf16[256,32,128]{2,1,0:T(8,128)(2,1)S(1)}, u32[]{:S(2)}, u32[]{:S(2)}) async-start(bf16[256,32,128]{2,1,0:T(8,128)(2,1)} %route.1), calls=%async_computation.1 | async-start | bytes 4194304 | tf_op jit(solution)/shard_map/all_to_all | solution.py:262
  59.6 2.2 %collective-permute-start = (bf16[2,16,4096]{2,1,0:T(8,128)(2,1)}, bf16[2,16,4096]{2,1,0:T(8,128)(2,1)S(1)}, u32[]{:S(2)}, u32[]{:S(2)}) collective-permute-start(bf16[2,16,4096]{2,1,0:T(8,128)(2,1)} %get-tuple-element.18), channel_id=1, source_target_pairs={{0,1},{1,0},{2,3},{3,2},{4,5},{5,4},{6,7},{7,6},{8,9},{9,8},{10,11... | collective-permute-start | bytes 786440 | tf_op jit(solution)/shard_map/ppermute | solution.py:237
  61.8 1.7 %collective-permute-start.2 = (bf16[2,16,4096]{2,1,0:T(8,128)(2,1)S(1)}, bf16[2,16,4096]{2,1,0:T(8,128)(2,1)S(1)}, u32[]{:S(2)}, u32[]{:S(2)}) collective-permute-start(bf16[2,16,4096]{2,1,0:T(8,128)(2,1)S(1)} %get-tuple-element.20), channel_id=1, source_target_pairs={{0,3},{1,2},{2,1},{3,0},{4,7},{5,6},{6,5},{7,4},{8,11},{9,10},{10,... | collective-permute-start | bytes 786440 | tf_op jit(solution)/shard_map/ppermute | solution.py:237
  63.6 11.0 %collective-permute-done.1.refs_2_ = bf16[2,16,4096]{2,1,0:T(8,128)(2,1)S(1)} collective-permute-done((bf16[2,16,4096]{2,1,0:T(8,128)(2,1)}, bf16[2,16,4096]{2,1,0:T(8,128)(2,1)S(1)}, u32[]{:S(2)}, u32[]{:S(2)}) %collective-permute-start.1) | collective-permute-done | bytes 262176 | tf_op jit(solution)/shard_map/ppermute | solution.py:237
  74.5 10.3 %collective-permute-done.2.refs_3_ = bf16[2,16,4096]{2,1,0:T(8,128)(2,1)S(1)} collective-permute-done((bf16[2,16,4096]{2,1,0:T(8,128)(2,1)S(1)}, bf16[2,16,4096]{2,1,0:T(8,128)(2,1)S(1)}, u32[]{:S(2)}, u32[]{:S(2)}) %collective-permute-start.2) | collective-permute-done | bytes 262176 | tf_op jit(solution)/shard_map/ppermute | solution.py:237
  84.8 26.8 %all-to-all-done.1.refs_4_ = bf16[256,32,128]{2,1,0:T(8,128)(2,1)S(1)} async-done(((bf16[256,32,128]{2,1,0:T(8,128)(2,1)}), bf16[256,32,128]{2,1,0:T(8,128)(2,1)S(1)}, u32[]{:S(2)}, u32[]{:S(2)}) %all-to-all-start.1) | async-done | bytes 2097184 | tf_op jit(solution)/shard_map/all_to_all | solution.py:262
  111.7 0.9 copy-done.2
  112.6 0.9 copy-done.4
  113.5 0.8 copy-done.5
  114.3 6.6 %solve.3 = (bf16[16,4096]{1,0:T(8,128)(2,1)S(1)}, bf16[16,4096]{1,0:T(8,128)(2,1)S(1)}, bf16[16,4096]{1,0:T(8,128)(2,1)S(1)}, bf16[16,4096]{1,0:T(8,128)(2,1)S(1)}) custom-call(s32[1]{0:T(128)} %bitcast.q_ref, bf16[2,16,4096]{2,1,0:T(8,128)(2,1)S(1)} %get-tuple-element.17.refs_0_, bf16[2,16,4096]{2,1,0:T(8,128)(2,1)S(1)} %collective-permute-done.refs_1_, ...), custom_call_target="tpu_custom_call" | custom-call | flops 10000000000 | bytes 8000000 | tf_op jit(solution)/shard_map/solve/pallas_call | solution.py:268
  120.9 0.7 collective-permute-start.6
  121.6 0.5 collective-permute-start.7
  122.1 1.2 collective-permute-start.8
  123.3 6.6 %solve.2 = (bf16[16,4096]{1,0:T(8,128)(2,1)S(1)}, bf16[16,4096]{1,0:T(8,128)(2,1)S(1)}, bf16[16,4096]{1,0:T(8,128)(2,1)S(1)}, bf16[16,4096]{1,0:T(8,128)(2,1)S(1)}) custom-call(s32[1]{0:T(128)} %bitcast.q_ref, bf16[2,16,4096]{2,1,0:T(8,128)(2,1)S(1)} %get-tuple-element.17.refs_0_, bf16[2,16,4096]{2,1,0:T(8,128)(2,1)S(1)} %collective-permute-done.refs_1_, ...), custom_call_target="tpu_custom_call" | custom-call | flops 10000000000 | bytes 8000000 | tf_op jit(solution)/shard_map/solve/pallas_call | solution.py:268
  129.9 0.2 collective-permute-start.3
  130.2 0.5 collective-permute-start.4
  130.7 1.5 %collective-permute-start.5 = (bf16[16,4096]{1,0:T(8,128)(2,1)S(1)}, bf16[16,4096]{1,0:T(8,128)(2,1)S(1)}, u32[]{:S(2)}, u32[]{:S(2)}) collective-permute-start(bf16[16,4096]{1,0:T(8,128)(2,1)S(1)} %get-tuple-element.25), channel_id=1, source_target_pairs={{0,3},{1,2},{2,1},{3,0},{4,7},{5,6},{6,5},{7,4},{8,11},{9,10},{10,... | collective-permute-start | bytes 393224 | tf_op jit(solution)/shard_map/ppermute | solution.py:237
  132.2 2.7 %collective-permute-done.4.refs_2_ = bf16[16,4096]{1,0:T(8,128)(2,1)S(1)} collective-permute-done((bf16[16,4096]{1,0:T(8,128)(2,1)S(1)}, bf16[16,4096]{1,0:T(8,128)(2,1)S(1)}, u32[]{:S(2)}, u32[]{:S(2)}) %collective-permute-start.4) | collective-permute-done | bytes 131104 | tf_op jit(solution)/shard_map/ppermute | solution.py:237
  134.9 3.3 %collective-permute-done.5.refs_3_ = bf16[16,4096]{1,0:T(8,128)(2,1)S(1)} collective-permute-done((bf16[16,4096]{1,0:T(8,128)(2,1)S(1)}, bf16[16,4096]{1,0:T(8,128)(2,1)S(1)}, u32[]{:S(2)}, u32[]{:S(2)}) %collective-permute-start.5) | collective-permute-done | bytes 131104 | tf_op jit(solution)/shard_map/ppermute | solution.py:237
  138.2 2.1 %assemble.1 = (f32[8,16,4096]{2,1,0:T(8,128)}, f32[8,8]{1,0:T(8,128)S(1)}) custom-call(s32[1]{0:T(128)} %bitcast.q_ref, f32[8,16,4096]{2,1,0:T(8,128)S(1)} %copy-done.1, bf16[16,4096]{1,0:T(8,128)(2,1)S(1)} %get-tuple-element.22.refs_0_, bf16[16,4096]{1,0:T(8,128)(2,1)S(1)} %collective-permute-done.3.refs_1_, ...), custom_call_target="tpu_custom_call" | custom-call | tf_op jit(solution)/shard_map/assemble/pallas_call | solution.py:282
  140.3 0.4 collective-permute-start.11
  140.7 0.9 collective-permute-start.10
  141.6 0.9 collective-permute-start.9
  142.4 0.9 collective-permute-done.11
  143.3 0.6 add_add_fusion
  (17 shorter events, 0.0 us)
Async XLA Ops:
  0.6 1.6 %copy-start = (f32[8,16,4096]{2,1,0:T(8,128)S(1)}, f32[8,16,4096]{2,1,0:T(8,128)}, u32[]{:S(2)}) copy-start(f32[8,16,4096]{2,1,0:T(8,128)} %orb_ref.3) | copy-start | bytes 6291460
  2.2 17.1 %copy-start.6 = (s32[8,2]{0,1:T(2,128)S(1)}, s32[8,2]{0,1:T(2,128)}, u32[]{:S(2)}) copy-start(s32[8,2]{0,1:T(2,128)} %param.10) | copy-start | bytes 196
  3.5 43.2 %all-to-all-start = ((bf16[64,64,128]{2,1,0:T(8,128)(2,1)}), bf16[64,64,128]{2,1,0:T(8,128)(2,1)S(1)}, u32[]{:S(2)}, u32[]{:S(2)}) async-start(bf16[64,64,128]{2,1,0:T(8,128)(2,1)} %get-tuple-element.21), calls=%async_computation | async-start | bytes 2097152 | tf_op jit(solution)/shard_map/all_to_all | solution.py:248
  50.6 61.0 %copy-start.3 = (bf16[4,64,192]{2,1,0:T(8,128)(2,1)S(1)}, bf16[4,64,192]{2,1,0:T(8,128)(2,1)}, u32[]{:S(2)}) copy-start(bf16[4,64,192]{2,1,0:T(8,128)(2,1)} %constant.15.clone.refs_6_) | copy-start | bytes 294916
  50.6 61.0 %all-to-all-start.1 = ((bf16[256,32,128]{2,1,0:T(8,128)(2,1)}), bf16[256,32,128]{2,1,0:T(8,128)(2,1)S(1)}, u32[]{:S(2)}, u32[]{:S(2)}) async-start(bf16[256,32,128]{2,1,0:T(8,128)(2,1)} %route.1), calls=%async_computation.1 | async-start | bytes 4194304 | tf_op jit(solution)/shard_map/all_to_all | solution.py:262
  59.6 4.0 %collective-permute-start = (bf16[2,16,4096]{2,1,0:T(8,128)(2,1)}, bf16[2,16,4096]{2,1,0:T(8,128)(2,1)S(1)}, u32[]{:S(2)}, u32[]{:S(2)}) collective-permute-start(bf16[2,16,4096]{2,1,0:T(8,128)(2,1)} %get-tuple-element.18), channel_id=1, source_target_pairs={{0,1},{1,0},{2,3},{3,2},{4,5},{5,4},{6,7},{7,6},{8,9},{9,8},{10,11... | collective-permute-start | bytes 786440 | tf_op jit(solution)/shard_map/ppermute | solution.py:237
  61.8 12.7 %collective-permute-start.1 = (bf16[2,16,4096]{2,1,0:T(8,128)(2,1)}, bf16[2,16,4096]{2,1,0:T(8,128)(2,1)S(1)}, u32[]{:S(2)}, u32[]{:S(2)}) collective-permute-start(bf16[2,16,4096]{2,1,0:T(8,128)(2,1)} %get-tuple-element.19), channel_id=1, source_target_pairs={{0,2},{1,3},{2,0},{3,1},{4,6},{5,7},{6,4},{7,5},{8,10},{9,11},{10,... | collective-permute-start | bytes 786440 | tf_op jit(solution)/shard_map/ppermute | solution.py:237
  61.8 23.0 %collective-permute-start.2 = (bf16[2,16,4096]{2,1,0:T(8,128)(2,1)S(1)}, bf16[2,16,4096]{2,1,0:T(8,128)(2,1)S(1)}, u32[]{:S(2)}, u32[]{:S(2)}) collective-permute-start(bf16[2,16,4096]{2,1,0:T(8,128)(2,1)S(1)} %get-tuple-element.20), channel_id=1, source_target_pairs={{0,3},{1,2},{2,1},{3,0},{4,7},{5,6},{6,5},{7,4},{8,11},{9,10},{10,... | collective-permute-start | bytes 786440 | tf_op jit(solution)/shard_map/ppermute | solution.py:237
  111.7 1.0 copy-start.2
  112.6 0.9 copy-start.4
  113.5 0.8 copy-start.5
  120.9 9.9 %collective-permute-start.6 = (bf16[16,4096]{1,0:T(8,128)(2,1)S(1)}, bf16[16,4096]{1,0:T(8,128)(2,1)S(1)}, u32[]{:S(2)}, u32[]{:S(2)}) collective-permute-start(bf16[16,4096]{1,0:T(8,128)(2,1)S(1)} %get-tuple-element.27), channel_id=1, source_target_pairs={{0,1},{1,0},{2,3},{3,2},{4,5},{5,4},{6,7},{7,6},{8,9},{9,8},{10,11... | collective-permute-start | bytes 393224 | tf_op jit(solution)/shard_map/ppermute | solution.py:237
  121.6 10.6 %collective-permute-start.7 = (bf16[16,4096]{1,0:T(8,128)(2,1)S(1)}, bf16[16,4096]{1,0:T(8,128)(2,1)S(1)}, u32[]{:S(2)}, u32[]{:S(2)}) collective-permute-start(bf16[16,4096]{1,0:T(8,128)(2,1)S(1)} %get-tuple-element.28), channel_id=1, source_target_pairs={{0,2},{1,3},{2,0},{3,1},{4,6},{5,7},{6,4},{7,5},{8,10},{9,11},{10,... | collective-permute-start | bytes 393224 | tf_op jit(solution)/shard_map/ppermute | solution.py:237
  122.1 16.1 %copy-start.1 = (f32[8,16,4096]{2,1,0:T(8,128)S(1)}, f32[8,16,4096]{2,1,0:T(8,128)}, u32[]{:S(2)}) copy-start(f32[8,16,4096]{2,1,0:T(8,128)} %orb_ref.3) | copy-start | bytes 6291460
  122.1 10.1 %collective-permute-start.8 = (bf16[16,4096]{1,0:T(8,128)(2,1)S(1)}, bf16[16,4096]{1,0:T(8,128)(2,1)S(1)}, u32[]{:S(2)}, u32[]{:S(2)}) collective-permute-start(bf16[16,4096]{1,0:T(8,128)(2,1)S(1)} %get-tuple-element.29), channel_id=1, source_target_pairs={{0,3},{1,2},{2,1},{3,0},{4,7},{5,6},{6,5},{7,4},{8,11},{9,10},{10,... | collective-permute-start | bytes 393224 | tf_op jit(solution)/shard_map/ppermute | solution.py:237
  129.9 2.2 %collective-permute-start.3 = (bf16[16,4096]{1,0:T(8,128)(2,1)S(1)}, bf16[16,4096]{1,0:T(8,128)(2,1)S(1)}, u32[]{:S(2)}, u32[]{:S(2)}) collective-permute-start(bf16[16,4096]{1,0:T(8,128)(2,1)S(1)} %get-tuple-element.23), channel_id=1, source_target_pairs={{0,1},{1,0},{2,3},{3,2},{4,5},{5,4},{6,7},{7,6},{8,9},{9,8},{10,11... | collective-permute-start | bytes 393224 | tf_op jit(solution)/shard_map/ppermute | solution.py:237
  130.2 4.7 %collective-permute-start.4 = (bf16[16,4096]{1,0:T(8,128)(2,1)S(1)}, bf16[16,4096]{1,0:T(8,128)(2,1)S(1)}, u32[]{:S(2)}, u32[]{:S(2)}) collective-permute-start(bf16[16,4096]{1,0:T(8,128)(2,1)S(1)} %get-tuple-element.24), channel_id=1, source_target_pairs={{0,2},{1,3},{2,0},{3,1},{4,6},{5,7},{6,4},{7,5},{8,10},{9,11},{10,... | collective-permute-start | bytes 393224 | tf_op jit(solution)/shard_map/ppermute | solution.py:237
  130.7 7.5 %collective-permute-start.5 = (bf16[16,4096]{1,0:T(8,128)(2,1)S(1)}, bf16[16,4096]{1,0:T(8,128)(2,1)S(1)}, u32[]{:S(2)}, u32[]{:S(2)}) collective-permute-start(bf16[16,4096]{1,0:T(8,128)(2,1)S(1)} %get-tuple-element.25), channel_id=1, source_target_pairs={{0,3},{1,2},{2,1},{3,0},{4,7},{5,6},{6,5},{7,4},{8,11},{9,10},{10,... | collective-permute-start | bytes 393224 | tf_op jit(solution)/shard_map/ppermute | solution.py:237
  140.3 3.0 %collective-permute-start.11 = (f32[8,8]{1,0:T(8,128)S(1)}, f32[8,8]{1,0:T(8,128)S(1)}, u32[]{:S(2)}, u32[]{:S(2)}) collective-permute-start(f32[8,8]{1,0:T(8,128)S(1)} %get-tuple-element.31), channel_id=1, source_target_pairs={{0,3},{1,2},{2,1},{3,0},{4,7},{5,6},{6,5},{7,4},{8,11},{9,10},{10,... | collective-permute-start | bytes 776 | tf_op jit(solution)/shard_map/ppermute | solution.py:237
  140.7 2.7 %collective-permute-start.10 = (f32[8,8]{1,0:T(8,128)S(1)}, f32[8,8]{1,0:T(8,128)S(1)}, u32[]{:S(2)}, u32[]{:S(2)}) collective-permute-start(f32[8,8]{1,0:T(8,128)S(1)} %get-tuple-element.31), channel_id=1, source_target_pairs={{0,2},{1,3},{2,0},{3,1},{4,6},{5,7},{6,4},{7,5},{8,10},{9,11},{10,... | collective-permute-start | bytes 776 | tf_op jit(solution)/shard_map/ppermute | solution.py:237
  141.6 1.8 %collective-permute-start.9 = (f32[8,8]{1,0:T(8,128)S(1)}, f32[8,8]{1,0:T(8,128)S(1)}, u32[]{:S(2)}, u32[]{:S(2)}) collective-permute-start(f32[8,8]{1,0:T(8,128)S(1)} %get-tuple-element.31), channel_id=1, source_target_pairs={{0,1},{1,0},{2,3},{3,2},{4,5},{5,4},{6,7},{7,6},{8,9},{9,8},{10,11... | collective-permute-start | bytes 776 | tf_op jit(solution)/shard_map/ppermute | solution.py:237

commit v2 on v1

--- a/solution.py
+++ b/solution.py
@@ -1,3 +1,4 @@
+import functools
 import math
 
 import jax
@@ -21,10 +22,18 @@
 PITCH = 72
 SUB = 8
 SPOTS = 64
+STEPS = 4
+X_FORWARD = 0
+X_BACK = 256
+Z_FORWARD = 512
+Z_BACK = 1024
+Y_BOTH = 1536
+ROWS = 4096
 VMEM_LIMIT = 48 * 1024 * 1024
 
 VMEM = pl.BlockSpec(memory_space=pltpu.VMEM)
 SMEM = pl.BlockSpec(memory_space=pltpu.SMEM)
+HBM = pl.BlockSpec(memory_space=pltpu.HBM)
 
 
 def cas_matrix():
@@ -66,7 +75,13 @@
     total = squares[:, None, None] + squares[None, :, None] + squares[None, None, :]
     kernel = 1.0 / (total + SCREEN) / N**3
     kernel = np.concatenate([kernel, kernel], axis=-1).astype(np.float32)
-    return x_forward, x_back, y_both, z_forward, z_back, kernel
+    packed = np.zeros((ROWS, 4 * N), ml_dtypes.bfloat16)
+    packed[X_FORWARD : X_FORWARD + PAIR * N, : 3 * N] = x_forward.reshape(PAIR * N, 3 * N)
+    packed[X_BACK : X_BACK + PAIR * N, : 3 * N] = x_back.reshape(PAIR * N, 3 * N)
+    packed[Z_FORWARD : Z_FORWARD + 8 * N] = z_forward.reshape(8 * N, 4 * N)
+    packed[Z_BACK : Z_BACK + 8 * N] = z_back.reshape(8 * N, 4 * N)
+    packed[Y_BOTH : Y_BOTH + N, : 3 * N] = y_both
+    return packed, kernel
 
 
 def arrange(q_ref, orb_ref, spread_ref, *own):
@@ -88,20 +103,30 @@
         give_ref[first] = second
         take_ref[second] = first
 
-    @pl.loop(0, SPOTS, unroll=4)
-    def _(j):
-        wide[j] = held_ref[j].astype(jnp.float32).reshape(BLK, SUB, 128)
-
-    @pl.loop(0, SPOTS)
-    def _(b):
-        below = lax.rem(b - offset_ref[0] + SPOTS, SPOTS)
-        above = lax.rem(b + offset_ref[0], SPOTS)
+    gives = [give_ref[band] * SUB for band in range(BLK)]
+    takes = [take_ref[band] * SUB for band in range(BLK)]
+    offset = offset_ref[0]
+
+    def picked(start):
+        return wide[pl.ds(pl.multiple_of(start, SUB), SUB), :]
+
+    @pl.when(pl.program_id(0) == 0)
+    def _():
+        @pl.loop(0, SPOTS, unroll=4)
+        def _(j):
+            at = pl.ds(pl.multiple_of(j * BLK * SUB, BLK * SUB), BLK * SUB)
+            wide[at, :] = held_ref[j].astype(jnp.float32)
+
+    @pl.loop(0, SPOTS // STEPS, unroll=4)
+    def _(at):
+        b = pl.program_id(0) * (SPOTS // STEPS) + at
+        below = ((b - offset) & (SPOTS - 1)) * (BLK * SUB)
+        above = ((b + offset) & (SPOTS - 1)) * (BLK * SUB)
         for q in range(PAIR):
             rows = []
-            for i in range(2):
-                rows.append(wide[below, give_ref[q * 2 + i]])
-                rows.append(wide[above, take_ref[q * 2 + i]])
-            out_ref[b * PAIR + q] = jnp.concatenate(rows, axis=0).astype(jnp.bfloat16)
+            for band in (q * 2, q * 2 + 1):
+                rows += [picked(below + gives[band]), picked(above + takes[band])]
+            out_ref[at * PAIR + q] = jnp.concatenate(rows, axis=0).astype(jnp.bfloat16)
 
 
 def split(value):
@@ -118,27 +143,47 @@
 
 def right_dot(value, table_ref):
     high, low = split(value)
-    out = jnp.dot(high, table_ref[0], preferred_element_type=jnp.float32)
-    out += jnp.dot(low, table_ref[0], preferred_element_type=jnp.float32)
-    out += jnp.dot(high, table_ref[1], preferred_element_type=jnp.float32)
+    out = jnp.dot(high, table_ref[: 4 * N], preferred_element_type=jnp.float32)
+    out += jnp.dot(low, table_ref[: 4 * N], preferred_element_type=jnp.float32)
+    out += jnp.dot(high, table_ref[4 * N :], preferred_element_type=jnp.float32)
     return out
 
 
-def solve(q_ref, *refs):
+def solve(a, q_ref, *refs):
     own, seen = refs[0:4], refs[4]
-    xf_ref, xb_ref, y_ref, zf_ref, zb_ref, k_ref = refs[5:11]
-    outs, work = refs[11:15], refs[15]
+    packed, kernel, outs, work = refs[5], refs[6], refs[7:11], refs[11]
+    xf_ref, zf_ref, y_ref, k_ref, zb_ref, xb_ref = rooms = refs[12:18]
+    sems = refs[18]
     q = q_ref[0]
     cast = jnp.float32
+    here = pl.multiple_of(q * N, N)
+    sources = (
+        packed.at[pl.ds(X_FORWARD + here, N)],
+        packed.at[pl.ds(Z_FORWARD, 8 * N)],
+        packed.at[pl.ds(Y_BOTH, N)],
+        kernel,
+        packed.at[pl.ds(Z_BACK, 8 * N)],
+        packed.at[pl.ds(X_BACK + here, N)],
+    )
+    loads = [
+        pltpu.make_async_copy(source, room, sems.at[n])
+        for n, (source, room) in enumerate(zip(sources, rooms))
+    ]
+    for load in loads:
+        load.start()
+    rows_at = slice(a * 2 * SUB, (a + 1) * 2 * SUB)
 
     def visiting(tile):
         below, above = [], []
         for h in range(2):
             for d in range(PAIR):
-                rows = seen[(tile * 2 + h) * PAIR + (q ^ d)].astype(cast)
+                rows = seen[(tile * 2 + h) * PAIR + (q ^ d), rows_at].astype(cast)
                 below.append(rows[:SUB])
                 above.append(rows[SUB:])
         return jnp.concatenate(below, axis=0), jnp.concatenate(above, axis=0)
+
+    loads[0].wait()
+    loads[1].wait()
 
     @pl.loop(0, LANES // CHUNK)
     def _(c):
@@ -146,13 +191,13 @@
         for t in range(TILES):
             tile = c * TILES + t
             at = pl.ds(pl.multiple_of(tile * 128, 128), 128)
-            slabs = [own[d][0, :, at].astype(cast) for d in range(PAIR)]
+            slabs = [own[d][a, :, at].astype(cast) for d in range(PAIR)]
             mine = jnp.concatenate(
                 [slabs[d][h * SUB : h * SUB + SUB] for h in range(2) for d in range(PAIR)], axis=0
             )
             below, above = visiting(tile)
             wide += [mine * below, mine * above]
-        done_x = left_dot(xf_ref[q], jnp.concatenate(wide, axis=1))
+        done_x = left_dot(xf_ref[:, : 3 * N], jnp.concatenate(wide, axis=1))
         tall = jnp.concatenate(
             [done_x[:, t * 256 : t * 256 + 256] for t in range(TILES)], axis=0
         )
@@ -163,15 +208,21 @@
             work[pl.ds(pl.multiple_of(y * PITCH, 8), N), :] = part[:, :128]
             work[pl.ds(pl.multiple_of(y * PITCH + PITCH, 8), N), :] = part[:, 128:]
 
+    loads[2].wait()
+    loads[3].wait()
+
     @pl.loop(0, N // XSTEP)
     def _(step):
         spots = [step * XSTEP + i for i in range(XSTEP)]
         value = jnp.concatenate([work[pl.ds(x, N, stride=PITCH), :] for x in spots], axis=1)
-        value = left_dot(y_ref[...], value)
+        value = left_dot(y_ref[:, : 3 * N], value)
         weight = jnp.concatenate([k_ref[x] for x in spots], axis=1)
-        value = left_dot(y_ref[...], value * weight)
+        value = left_dot(y_ref[:, : 3 * N], value * weight)
         for i, x in enumerate(spots):
             work[pl.ds(x, N, stride=PITCH), :] = value[:, i * 128 : i * 128 + 128]
+
+    loads[4].wait()
+    loads[5].wait()
 
     @pl.loop(0, LANES // CHUNK)
     def _(c):
@@ -183,7 +234,7 @@
             parts.append(jnp.concatenate([even, odd], axis=1))
         done_z = right_dot(jnp.concatenate(parts, axis=0), zb_ref)
         wide = jnp.concatenate([done_z[t * N : t * N + N] for t in range(TILES)], axis=1)
-        pot = left_dot(xb_ref[q], wide)
+        pot = left_dot(xb_ref[:, : 3 * N], wide)
         for t in range(TILES):
             tile = c * TILES + t
             at = pl.ds(pl.multiple_of(tile * 128, 128), 128)
@@ -197,14 +248,13 @@
                 outs[d][:, at] = jnp.concatenate(rows, axis=0).astype(jnp.bfloat16)
 
 
-def assemble(q_ref, orb_ref, *refs):
-    parts, field_ref, gram_ref, flat = refs[0:8], refs[8], refs[9], refs[10]
+def overlap(q_ref, orb_ref, *refs):
+    parts, gram_ref, flat = refs[0:8], refs[8], refs[9]
     for d in range(PAIR):
         base = (q_ref[0] ^ d) * 2
         for i in range(2):
-            rows = parts[i * PAIR + d][...]
-            field_ref[base + i] = rows.astype(jnp.float32)
-            flat[pl.ds(pl.multiple_of((base + i) * SLAB, SLAB), SLAB), :] = rows
+            at = pl.ds(pl.multiple_of((base + i) * SLAB, SLAB), SLAB)
+            flat[at, :] = parts[i * PAIR + d][...]
     rows = BLK * SLAB
     high, low = split(orb_ref[...].reshape(rows, LANES))
     dims = (((1,), (1,)), ((), ()))
@@ -225,6 +275,14 @@
     ) / math.sqrt(N**3)
 
 
+def widen(q_ref, *refs):
+    parts, field_ref = refs[0:8], refs[8]
+    for d in range(PAIR):
+        base = (q_ref[0] ^ d) * 2
+        for i in range(2):
+            field_ref[base + i] = parts[i * PAIR + d][...].astype(jnp.float32)
+
+
 PARAMS = pltpu.CompilerParams(vmem_limit_bytes=VMEM_LIMIT)
 PIECE = jax.ShapeDtypeStruct((2, SLAB, LANES), jnp.bfloat16)
 SENT = jax.ShapeDtypeStruct((SLAB, LANES), jnp.bfloat16)
@@ -249,10 +307,11 @@
     routed = pl.pallas_call(
         route,
         out_shape=jax.ShapeDtypeStruct((SPOTS * PAIR, 4 * SUB, 128), jnp.bfloat16),
+        grid=(STEPS,),
         in_specs=[SMEM, SMEM, VMEM],
-        out_specs=VMEM,
+        out_specs=pl.BlockSpec((SPOTS * PAIR // STEPS, 4 * SUB, 128), lambda i: (i, 0, 0)),
         scratch_shapes=[
-            pltpu.VMEM((SPOTS, BLK, SUB, 128), jnp.float32),
+            pltpu.VMEM((SPOTS * BLK * SUB, 128), jnp.float32),
             pltpu.SMEM((BLK,), jnp.int32),
             pltpu.SMEM((BLK,), jnp.int32),
         ],
@@ -263,35 +322,44 @@
     consts = [jnp.asarray(t) for t in tables()]
     back = []
     for a in range(2):
-        one = pl.BlockSpec((1, SLAB, LANES), lambda i, a=a: (a, 0, 0))
-        rows = pl.BlockSpec((SPOTS * PAIR, 2 * SUB, 128), lambda i, a=a: (0, a, 0))
         sent = pl.pallas_call(
-            solve,
-            grid=(1,),
+            functools.partial(solve, a),
             out_shape=[SENT] * 4,
-            in_specs=[SMEM] + [one] * 4 + [rows] + [VMEM] * 6,
+            in_specs=[SMEM] + [VMEM] * 5 + [HBM] * 2,
             out_specs=[VMEM] * 4,
-            scratch_shapes=[pltpu.VMEM((N * PITCH, 128), jnp.float32)],
-            compiler_params=PARAMS,
+            scratch_shapes=[pltpu.VMEM((N * PITCH, 128), jnp.float32)]
+            + [
+                pltpu.VMEM((rows, 4 * N), jnp.bfloat16) if rows else pltpu.VMEM((N, N, 2 * N), jnp.float32)
+                for rows in (N, 8 * N, N, 0, 8 * N, N)
+            ]
+            + [pltpu.SemaphoreType.DMA((6,))],
+            compiler_params=pltpu.CompilerParams(vmem_limit_bytes=50 * 1024 * 1024),
             cost_estimate=pl.CostEstimate(
                 flops=10_000_000_000, bytes_accessed=8_000_000, transcendentals=0
             ),
             name="solve",
         )(q, *own, seen, *consts)
         back += [sent[0]] + [across(sent[d], d) for d in range(1, PAIR)]
-    field, gram = pl.pallas_call(
-        assemble,
-        out_shape=[
-            jax.ShapeDtypeStruct((BLK, SLAB, LANES), jnp.float32),
-            jax.ShapeDtypeStruct((BLK, BLK), jnp.float32),
-        ],
+    gram = pl.pallas_call(
+        overlap,
+        out_shape=jax.ShapeDtypeStruct((BLK, BLK), jnp.float32),
         in_specs=[SMEM] + [VMEM] * 9,
-        out_specs=[VMEM] * 2,
+        out_specs=VMEM,
         scratch_shapes=[pltpu.VMEM((BLK * SLAB, LANES), jnp.bfloat16)],
         compiler_params=PARAMS,
-        name="assemble",
+        name="overlap",
     )(q, orbitals, *back)
-    return field, (gram + across(gram, 1)) + (across(gram, 2) + across(gram, 3))
+    others = [across(gram, d) for d in range(1, PAIR)]
+    field = pl.pallas_call(
+        widen,
+        out_shape=jax.ShapeDtypeStruct((BLK, SLAB, LANES), jnp.float32),
+        in_specs=[SMEM] + [VMEM] * 8,
+        out_specs=VMEM,
+        compiler_params=PARAMS,
+        cost_estimate=pl.CostEstimate(flops=0, bytes_accessed=8_000_000, transcendentals=0),
+        name="widen",
+    )(q, *back)
+    return field, (gram + others[0]) + (others[1] + others[2])
 
 
 def solution(mesh):

time: 144 us -> 139 us (0.965)
  local copies, waits for them, and re-layouts: 4.29 us -> 1.68 us
  Pallas kernels: 20.5 us -> 19 us
    unnamed x15 -> x7, local copies, waits for them, and re-layouts: 4.29 us -> 1.68 us
    pallas_call x3 -> x4, Pallas kernels: 15.3 us -> 14.5 us  [the longest x2 12 us: on_device(): pl.pallas_call(functools.partial(solve, a), out_shape=[SENT] * 4, in_spec...]
  transfers between devices with their start and end apart: 14 -> 14, of which waited for: 7 -> 6; matrix products, arithmetic and copies ran while one was open for 0% -> 0% of each run, Pallas kernels for 5% -> 5%
where the time goes in v2:
time: 139 us
  waiting for transfers between devices  81.4 us (59%)
  starting transfers between devices  34.9 us (25%)
  Pallas kernels  19 us (14%)
  local copies, waits for them, and re-layouts  1.68 us (1%)
    all_to_all x1, waiting for transfers between devices, on_device(): held = lax.all_to_all(spread, 'band', 0, 0, tiled=True)  27.3 us
    ppermute x12, waiting for transfers between devices, across(): return lax.ppermute(value, 'pair', [(i, i ^ d) for i in range(PAIR)])  27.3 us
    all_to_all x1, waiting for transfers between devices, on_device(): seen = lax.all_to_all(routed, ('band', 'pair'), 0, 0, tiled=True)  26.8 us
    all_to_all x1, starting transfers between devices, on_device(): held = lax.all_to_all(spread, 'band', 0, 0, tiled=True)  15.1 us
    pallas_call x2, Pallas kernels, on_device(): pl.pallas_call(functools.partial(solve, a), out_shape=[SENT] * 4, in_spec...  12 us
    ppermute x12, starting transfers between devices, across(): return lax.ppermute(value, 'pair', [(i, i ^ d) for i in range(PAIR)])  10.8 us
    all_to_all x1, starting transfers between devices, on_device(): seen = lax.all_to_all(routed, ('band', 'pair'), 0, 0, tiled=True)  8.97 us
    pallas_call x1, Pallas kernels, on_device(): pl.pallas_call(route, out_shape=jax.ShapeDtypeStruct((SPOTS * PAIR, 4 * S...  3.25 us
  transfers between devices with their start and end apart: 14, of which 6 were waited for; matrix products, arithmetic and copies ran while one was open for 0% of the time, Pallas kernels for 5%

profile of v2, /device:TPU:1, one launch (start us, length us, event | category | flops | bytes accessed | tf_op | source)
XLA Modules:
  0.0 139.0 jit_solution(928790262510759672)
XLA Ops:
  0.6 0.0 copy-start
  0.6 1.6 %copy-done = f32[8,16,4096]{2,1,0:T(8,128)S(1)} copy-done((f32[8,16,4096]{2,1,0:T(8,128)S(1)}, f32[8,16,4096]{2,1,0:T(8,128)}, u32[]{:S(2)}) %copy-start) | copy-done | bytes 2097176
  2.2 1.3 arrange.1
  3.5 15.1 %all-to-all-start = ((bf16[64,64,128]{2,1,0:T(8,128)(2,1)}), bf16[64,64,128]{2,1,0:T(8,128)(2,1)S(1)}, u32[]{:S(2)}, u32[]{:S(2)}) async-start(bf16[64,64,128]{2,1,0:T(8,128)(2,1)} %get-tuple-element.19), calls=%async_computation | async-start | bytes 2097152 | tf_op jit(solution)/shard_map/all_to_all | solution.py:306
  19.3 0.1 copy.7.table_ref
  19.4 27.3 %all-to-all-done.held_ref = bf16[64,64,128]{2,1,0:T(8,128)(2,1)S(1)} async-done(((bf16[64,64,128]{2,1,0:T(8,128)(2,1)}), bf16[64,64,128]{2,1,0:T(8,128)(2,1)S(1)}, u32[]{:S(2)}, u32[]{:S(2)}) %all-to-all-start) | async-done | bytes 1048608 | tf_op jit(solution)/shard_map/all_to_all | solution.py:306
  46.7 3.3 %route.1 = bf16[256,32,128]{2,1,0:T(8,128)(2,1)} custom-call(s32[8,2]{1,0:T(8,128)S(1)} %copy.7.table_ref, s32[1]{0:T(128)S(6)} %copy.8.offset_ref, bf16[64,64,128]{2,1,0:T(8,128)(2,1)S(1)} %all-to-all-done.held_ref), custom_call_target="tpu_custom_call" | custom-call | tf_op jit(solution)/shard_map/route/pallas_call | solution.py:307
  49.9 9.0 %all-to-all-start.1 = ((bf16[256,32,128]{2,1,0:T(8,128)(2,1)}), bf16[256,32,128]{2,1,0:T(8,128)(2,1)S(1)}, u32[]{:S(2)}, u32[]{:S(2)}) async-start(bf16[256,32,128]{2,1,0:T(8,128)(2,1)} %route.1), calls=%async_computation.1 | async-start | bytes 4194304 | tf_op jit(solution)/shard_map/all_to_all | solution.py:321
  58.9 2.2 %collective-permute-start = (bf16[2,16,4096]{2,1,0:T(8,128)(2,1)}, bf16[2,16,4096]{2,1,0:T(8,128)(2,1)S(1)}, u32[]{:S(2)}, u32[]{:S(2)}) collective-permute-start(bf16[2,16,4096]{2,1,0:T(8,128)(2,1)} %get-tuple-element.16), channel_id=1, source_target_pairs={{0,1},{1,0},{2,3},{3,2},{4,5},{5,4},{6,7},{7,6},{8,9},{9,8},{10,11... | collective-permute-start | bytes 786440 | tf_op jit(solution)/shard_map/ppermute | solution.py:295
  61.1 1.7 %collective-permute-start.2 = (bf16[2,16,4096]{2,1,0:T(8,128)(2,1)S(1)}, bf16[2,16,4096]{2,1,0:T(8,128)(2,1)S(1)}, u32[]{:S(2)}, u32[]{:S(2)}) collective-permute-start(bf16[2,16,4096]{2,1,0:T(8,128)(2,1)S(1)} %get-tuple-element.18), channel_id=1, source_target_pairs={{0,3},{1,2},{2,1},{3,0},{4,7},{5,6},{6,5},{7,4},{8,11},{9,10},{10,... | collective-permute-start | bytes 786440 | tf_op jit(solution)/shard_map/ppermute | solution.py:295
  62.9 11.0 %collective-permute-done.1.refs_2_ = bf16[2,16,4096]{2,1,0:T(8,128)(2,1)S(1)} collective-permute-done((bf16[2,16,4096]{2,1,0:T(8,128)(2,1)}, bf16[2,16,4096]{2,1,0:T(8,128)(2,1)S(1)}, u32[]{:S(2)}, u32[]{:S(2)}) %collective-permute-start.1) | collective-permute-done | bytes 262176 | tf_op jit(solution)/shard_map/ppermute | solution.py:295
  73.8 10.3 %collective-permute-done.2.refs_3_ = bf16[2,16,4096]{2,1,0:T(8,128)(2,1)S(1)} collective-permute-done((bf16[2,16,4096]{2,1,0:T(8,128)(2,1)S(1)}, bf16[2,16,4096]{2,1,0:T(8,128)(2,1)S(1)}, u32[]{:S(2)}, u32[]{:S(2)}) %collective-permute-start.2) | collective-permute-done | bytes 262176 | tf_op jit(solution)/shard_map/ppermute | solution.py:295
  84.1 26.8 %all-to-all-done.1.refs_4_ = bf16[256,32,128]{2,1,0:T(8,128)(2,1)S(1)} async-done(((bf16[256,32,128]{2,1,0:T(8,128)(2,1)}), bf16[256,32,128]{2,1,0:T(8,128)(2,1)S(1)}, u32[]{:S(2)}, u32[]{:S(2)}) %all-to-all-start.1) | async-done | bytes 2097184 | tf_op jit(solution)/shard_map/all_to_all | solution.py:321
  111.0 6.0 %solve.3 = (bf16[16,4096]{1,0:T(8,128)(2,1)S(1)}, bf16[16,4096]{1,0:T(8,128)(2,1)S(1)}, bf16[16,4096]{1,0:T(8,128)(2,1)S(1)}, bf16[16,4096]{1,0:T(8,128)(2,1)S(1)}) custom-call(s32[1]{0:T(128)} %bitcast.q_ref, bf16[2,16,4096]{2,1,0:T(8,128)(2,1)S(1)} %get-tuple-element.15.refs_0_, bf16[2,16,4096]{2,1,0:T(8,128)(2,1)S(1)} %collective-permute-done.refs_1_, ...), custom_call_target="tpu_custom_call" | custom-call | flops 10000000000 | bytes 8000000 | tf_op jit(solution)/shard_map/solve/pallas_call | solution.py:325
  117.0 0.7 collective-permute-start.6
  117.7 0.5 collective-permute-start.7
  118.2 1.2 collective-permute-start.8
  119.4 6.0 %solve.2 = (bf16[16,4096]{1,0:T(8,128)(2,1)S(1)}, bf16[16,4096]{1,0:T(8,128)(2,1)S(1)}, bf16[16,4096]{1,0:T(8,128)(2,1)S(1)}, bf16[16,4096]{1,0:T(8,128)(2,1)S(1)}) custom-call(s32[1]{0:T(128)} %bitcast.q_ref, bf16[2,16,4096]{2,1,0:T(8,128)(2,1)S(1)} %get-tuple-element.15.refs_0_, bf16[2,16,4096]{2,1,0:T(8,128)(2,1)S(1)} %collective-permute-done.refs_1_, ...), custom_call_target="tpu_custom_call" | custom-call | flops 10000000000 | bytes 8000000 | tf_op jit(solution)/shard_map/solve/pallas_call | solution.py:325
  125.4 0.2 collective-permute-start.3
  125.6 0.6 collective-permute-start.4
  126.2 0.0 collective-permute-done.6.refs_5_
  126.2 1.4 %collective-permute-start.5 = (bf16[16,4096]{1,0:T(8,128)(2,1)S(1)}, bf16[16,4096]{1,0:T(8,128)(2,1)S(1)}, u32[]{:S(2)}, u32[]{:S(2)}) collective-permute-start(bf16[16,4096]{1,0:T(8,128)(2,1)S(1)} %get-tuple-element.23), channel_id=1, source_target_pairs={{0,3},{1,2},{2,1},{3,0},{4,7},{5,6},{6,5},{7,4},{8,11},{9,10},{10,... | collective-permute-start | bytes 393224 | tf_op jit(solution)/shard_map/ppermute | solution.py:295
  127.6 0.0 collective-permute-done.7.refs_6_
  127.6 0.0 collective-permute-done.8.refs_7_
  127.6 2.7 %collective-permute-done.4.refs_2_ = bf16[16,4096]{1,0:T(8,128)(2,1)S(1)} collective-permute-done((bf16[16,4096]{1,0:T(8,128)(2,1)S(1)}, bf16[16,4096]{1,0:T(8,128)(2,1)S(1)}, u32[]{:S(2)}, u32[]{:S(2)}) %collective-permute-start.4) | collective-permute-done | bytes 131104 | tf_op jit(solution)/shard_map/ppermute | solution.py:295
  130.4 3.3 %collective-permute-done.5.refs_3_ = bf16[16,4096]{1,0:T(8,128)(2,1)S(1)} collective-permute-done((bf16[16,4096]{1,0:T(8,128)(2,1)S(1)}, bf16[16,4096]{1,0:T(8,128)(2,1)S(1)}, u32[]{:S(2)}, u32[]{:S(2)}) %collective-permute-start.5) | collective-permute-done | bytes 131104 | tf_op jit(solution)/shard_map/ppermute | solution.py:295
  133.7 1.1 overlap.1
  134.8 0.5 collective-permute-start.11
  135.3 0.7 collective-permute-start.10
  136.0 0.9 collective-permute-start.9
  136.9 1.5 %widen.1 = f32[8,16,4096]{2,1,0:T(8,128)} custom-call(s32[1]{0:T(128)} %bitcast.q_ref, bf16[16,4096]{1,0:T(8,128)(2,1)S(1)} %get-tuple-element.20.refs_0_, bf16[16,4096]{1,0:T(8,128)(2,1)S(1)} %collective-permute-done.3.refs_1_, bf16[16,4096]{1,0:T(8,128)(2,1)S(1)} %collective-permute-done.4.refs_2_, bf16[16,4096]{1,0:T(8,128)(2,1)S(1)} %collective-permute-done.5.refs_3_, ...), custom_call_target="tpu_custom_call" | custom-call | bytes 8000000 | tf_op jit(solution)/shard_map/widen/pallas_call | solution.py:353
  138.4 0.6 add_add_fusion
  (10 shorter events, 0.0 us)
Async XLA Ops:
  0.6 1.6 %copy-start = (f32[8,16,4096]{2,1,0:T(8,128)S(1)}, f32[8,16,4096]{2,1,0:T(8,128)}, u32[]{:S(2)}) copy-start(f32[8,16,4096]{2,1,0:T(8,128)} %orb_ref.3) | copy-start | bytes 6291460
  2.2 17.1 %copy-start.2 = (s32[8,2]{0,1:T(2,128)S(1)}, s32[8,2]{0,1:T(2,128)}, u32[]{:S(2)}) copy-start(s32[8,2]{0,1:T(2,128)} %param.6) | copy-start | bytes 196
  3.5 43.2 %all-to-all-start = ((bf16[64,64,128]{2,1,0:T(8,128)(2,1)}), bf16[64,64,128]{2,1,0:T(8,128)(2,1)S(1)}, u32[]{:S(2)}, u32[]{:S(2)}) async-start(bf16[64,64,128]{2,1,0:T(8,128)(2,1)} %get-tuple-element.19), calls=%async_computation | async-start | bytes 2097152 | tf_op jit(solution)/shard_map/all_to_all | solution.py:306
  49.9 61.0 %all-to-all-start.1 = ((bf16[256,32,128]{2,1,0:T(8,128)(2,1)}), bf16[256,32,128]{2,1,0:T(8,128)(2,1)S(1)}, u32[]{:S(2)}, u32[]{:S(2)}) async-start(bf16[256,32,128]{2,1,0:T(8,128)(2,1)} %route.1), calls=%async_computation.1 | async-start | bytes 4194304 | tf_op jit(solution)/shard_map/all_to_all | solution.py:321
  58.9 4.0 %collective-permute-start = (bf16[2,16,4096]{2,1,0:T(8,128)(2,1)}, bf16[2,16,4096]{2,1,0:T(8,128)(2,1)S(1)}, u32[]{:S(2)}, u32[]{:S(2)}) collective-permute-start(bf16[2,16,4096]{2,1,0:T(8,128)(2,1)} %get-tuple-element.16), channel_id=1, source_target_pairs={{0,1},{1,0},{2,3},{3,2},{4,5},{5,4},{6,7},{7,6},{8,9},{9,8},{10,11... | collective-permute-start | bytes 786440 | tf_op jit(solution)/shard_map/ppermute | solution.py:295
  61.1 12.7 %collective-permute-start.1 = (bf16[2,16,4096]{2,1,0:T(8,128)(2,1)}, bf16[2,16,4096]{2,1,0:T(8,128)(2,1)S(1)}, u32[]{:S(2)}, u32[]{:S(2)}) collective-permute-start(bf16[2,16,4096]{2,1,0:T(8,128)(2,1)} %get-tuple-element.17), channel_id=1, source_target_pairs={{0,2},{1,3},{2,0},{3,1},{4,6},{5,7},{6,4},{7,5},{8,10},{9,11},{10,... | collective-permute-start | bytes 786440 | tf_op jit(solution)/shard_map/ppermute | solution.py:295
  61.1 23.0 %collective-permute-start.2 = (bf16[2,16,4096]{2,1,0:T(8,128)(2,1)S(1)}, bf16[2,16,4096]{2,1,0:T(8,128)(2,1)S(1)}, u32[]{:S(2)}, u32[]{:S(2)}) collective-permute-start(bf16[2,16,4096]{2,1,0:T(8,128)(2,1)S(1)} %get-tuple-element.18), channel_id=1, source_target_pairs={{0,3},{1,2},{2,1},{3,0},{4,7},{5,6},{6,5},{7,4},{8,11},{9,10},{10,... | collective-permute-start | bytes 786440 | tf_op jit(solution)/shard_map/ppermute | solution.py:295
  117.0 9.3 %collective-permute-start.6 = (bf16[16,4096]{1,0:T(8,128)(2,1)S(1)}, bf16[16,4096]{1,0:T(8,128)(2,1)S(1)}, u32[]{:S(2)}, u32[]{:S(2)}) collective-permute-start(bf16[16,4096]{1,0:T(8,128)(2,1)S(1)} %get-tuple-element.25), channel_id=1, source_target_pairs={{0,1},{1,0},{2,3},{3,2},{4,5},{5,4},{6,7},{7,6},{8,9},{9,8},{10,11... | collective-permute-start | bytes 393224 | tf_op jit(solution)/shard_map/ppermute | solution.py:295
  117.7 10.0 %collective-permute-start.7 = (bf16[16,4096]{1,0:T(8,128)(2,1)S(1)}, bf16[16,4096]{1,0:T(8,128)(2,1)S(1)}, u32[]{:S(2)}, u32[]{:S(2)}) collective-permute-start(bf16[16,4096]{1,0:T(8,128)(2,1)S(1)} %get-tuple-element.26), channel_id=1, source_target_pairs={{0,2},{1,3},{2,0},{3,1},{4,6},{5,7},{6,4},{7,5},{8,10},{9,11},{10,... | collective-permute-start | bytes 393224 | tf_op jit(solution)/shard_map/ppermute | solution.py:295
  118.2 15.5 %copy-start.1 = (f32[8,16,4096]{2,1,0:T(8,128)S(1)}, f32[8,16,4096]{2,1,0:T(8,128)}, u32[]{:S(2)}) copy-start(f32[8,16,4096]{2,1,0:T(8,128)} %orb_ref.3) | copy-start | bytes 6291460
  118.2 9.5 %collective-permute-start.8 = (bf16[16,4096]{1,0:T(8,128)(2,1)S(1)}, bf16[16,4096]{1,0:T(8,128)(2,1)S(1)}, u32[]{:S(2)}, u32[]{:S(2)}) collective-permute-start(bf16[16,4096]{1,0:T(8,128)(2,1)S(1)} %get-tuple-element.27), channel_id=1, source_target_pairs={{0,3},{1,2},{2,1},{3,0},{4,7},{5,6},{6,5},{7,4},{8,11},{9,10},{10,... | collective-permute-start | bytes 393224 | tf_op jit(solution)/shard_map/ppermute | solution.py:295
  125.4 2.2 %collective-permute-start.3 = (bf16[16,4096]{1,0:T(8,128)(2,1)S(1)}, bf16[16,4096]{1,0:T(8,128)(2,1)S(1)}, u32[]{:S(2)}, u32[]{:S(2)}) collective-permute-start(bf16[16,4096]{1,0:T(8,128)(2,1)S(1)} %get-tuple-element.21), channel_id=1, source_target_pairs={{0,1},{1,0},{2,3},{3,2},{4,5},{5,4},{6,7},{7,6},{8,9},{9,8},{10,11... | collective-permute-start | bytes 393224 | tf_op jit(solution)/shard_map/ppermute | solution.py:295
  125.6 4.7 %collective-permute-start.4 = (bf16[16,4096]{1,0:T(8,128)(2,1)S(1)}, bf16[16,4096]{1,0:T(8,128)(2,1)S(1)}, u32[]{:S(2)}, u32[]{:S(2)}) collective-permute-start(bf16[16,4096]{1,0:T(8,128)(2,1)S(1)} %get-tuple-element.22), channel_id=1, source_target_pairs={{0,2},{1,3},{2,0},{3,1},{4,6},{5,7},{6,4},{7,5},{8,10},{9,11},{10,... | collective-permute-start | bytes 393224 | tf_op jit(solution)/shard_map/ppermute | solution.py:295
  126.2 7.4 %collective-permute-start.5 = (bf16[16,4096]{1,0:T(8,128)(2,1)S(1)}, bf16[16,4096]{1,0:T(8,128)(2,1)S(1)}, u32[]{:S(2)}, u32[]{:S(2)}) collective-permute-start(bf16[16,4096]{1,0:T(8,128)(2,1)S(1)} %get-tuple-element.23), channel_id=1, source_target_pairs={{0,3},{1,2},{2,1},{3,0},{4,7},{5,6},{6,5},{7,4},{8,11},{9,10},{10,... | collective-permute-start | bytes 393224 | tf_op jit(solution)/shard_map/ppermute | solution.py:295
  134.8 3.6 %collective-permute-start.11 = (f32[8,8]{1,0:T(8,128)S(1)}, f32[8,8]{1,0:T(8,128)S(1)}, u32[]{:S(2)}, u32[]{:S(2)}) collective-permute-start(f32[8,8]{1,0:T(8,128)S(1)} %overlap.1), channel_id=1, source_target_pairs={{0,3},{1,2},{2,1},{3,0},{4,7},{5,6},{6,5},{7,4},{8,11},{9,10},{10,... | collective-permute-start | bytes 776 | tf_op jit(solution)/shard_map/ppermute | solution.py:295
  135.3 3.1 %collective-permute-start.10 = (f32[8,8]{1,0:T(8,128)S(1)}, f32[8,8]{1,0:T(8,128)S(1)}, u32[]{:S(2)}, u32[]{:S(2)}) collective-permute-start(f32[8,8]{1,0:T(8,128)S(1)} %overlap.1), channel_id=1, source_target_pairs={{0,2},{1,3},{2,0},{3,1},{4,6},{5,7},{6,4},{7,5},{8,10},{9,11},{10,... | collective-permute-start | bytes 776 | tf_op jit(solution)/shard_map/ppermute | solution.py:295
  136.0 2.4 %collective-permute-start.9 = (f32[8,8]{1,0:T(8,128)S(1)}, f32[8,8]{1,0:T(8,128)S(1)}, u32[]{:S(2)}, u32[]{:S(2)}) collective-permute-start(f32[8,8]{1,0:T(8,128)S(1)} %overlap.1), channel_id=1, source_target_pairs={{0,1},{1,0},{2,3},{3,2},{4,5},{5,4},{6,7},{7,6},{8,9},{9,8},{10,11... | collective-permute-start | bytes 776 | tf_op jit(solution)/shard_map/ppermute | solution.py:295

commit v3 on v2

--- a/solution.py
+++ b/solution.py
@@ -25,10 +25,9 @@
 STEPS = 4
 X_FORWARD = 0
 X_BACK = 256
-Z_FORWARD = 512
-Z_BACK = 1024
-Y_BOTH = 1536
-ROWS = 4096
+Z_BOTH = 512
+Y_BOTH = 768
+ROWS = 832
 VMEM_LIMIT = 48 * 1024 * 1024
 
 VMEM = pl.BlockSpec(memory_space=pltpu.VMEM)
@@ -64,22 +63,19 @@
     x_forward = np.stack([three(cas[:, order[q]]) for q in range(PAIR)])
     x_back = np.stack([three(cas[order[q], :]) for q in range(PAIR)])
     y_both = three(cas)
-    weave = np.zeros((2, 2, N, 2, 2, N))
-    for source in range(2):
-        for parity in range(2):
-            weave[source, parity, :, parity, source, :] = cas
-    weave = weave.reshape(4 * N, 4 * N)
-    z_forward = np.stack(halves(weave))
-    z_back = np.stack(halves(weave.T.copy()))
+    pair = np.zeros((2 * N, 2 * N))
+    pair[:N, :N] = pair[N:, N:] = cas
+    high, low = halves(pair)
+    z_both = np.block([[high, low], [high, np.zeros_like(low)]])
     squares = 4.0 * np.sin(math.pi * np.arange(N) / N) ** 2
-    total = squares[:, None, None] + squares[None, :, None] + squares[None, None, :]
-    kernel = 1.0 / (total + SCREEN) / N**3
-    kernel = np.concatenate([kernel, kernel], axis=-1).astype(np.float32)
+    plane = squares[:, None] + squares[None, :] + SCREEN
+    plane = np.concatenate([plane, plane], axis=1)
+    kernel = np.concatenate([plane, np.repeat(squares[:, None], 2 * N, axis=1)])
+    kernel = (kernel * N**3).astype(np.float32)
     packed = np.zeros((ROWS, 4 * N), ml_dtypes.bfloat16)
     packed[X_FORWARD : X_FORWARD + PAIR * N, : 3 * N] = x_forward.reshape(PAIR * N, 3 * N)
     packed[X_BACK : X_BACK + PAIR * N, : 3 * N] = x_back.reshape(PAIR * N, 3 * N)
-    packed[Z_FORWARD : Z_FORWARD + 8 * N] = z_forward.reshape(8 * N, 4 * N)
-    packed[Z_BACK : Z_BACK + 8 * N] = z_back.reshape(8 * N, 4 * N)
+    packed[Z_BOTH : Z_BOTH + 4 * N] = z_both
     packed[Y_BOTH : Y_BOTH + N, : 3 * N] = y_both
     return packed, kernel
 
@@ -141,28 +137,34 @@
     return jnp.dot(table, stacked, preferred_element_type=jnp.float32)
 
 
-def right_dot(value, table_ref):
-    high, low = split(value)
-    out = jnp.dot(high, table_ref[: 4 * N], preferred_element_type=jnp.float32)
-    out += jnp.dot(low, table_ref[: 4 * N], preferred_element_type=jnp.float32)
-    out += jnp.dot(high, table_ref[4 * N :], preferred_element_type=jnp.float32)
-    return out
+def right_dot(value, table):
+    out = jnp.dot(
+        jnp.concatenate(split(value), axis=1), table, preferred_element_type=jnp.float32
+    )
+    return out[:, : 2 * N] + out[:, 2 * N :]
+
+
+def woven(first, second):
+    left = lax.broadcasted_iota(jnp.int32, first.shape, 1) < N
+    return (
+        jnp.where(left, first, pltpu.roll(second, N, 1)),
+        jnp.where(left, pltpu.roll(first, N, 1), second),
+    )
 
 
 def solve(a, q_ref, *refs):
     own, seen = refs[0:4], refs[4]
     packed, kernel, outs, work = refs[5], refs[6], refs[7:11], refs[11]
-    xf_ref, zf_ref, y_ref, k_ref, zb_ref, xb_ref = rooms = refs[12:18]
-    sems = refs[18]
+    xf_ref, z_ref, y_ref, k_ref, xb_ref = rooms = refs[12:17]
+    sems = refs[17]
     q = q_ref[0]
     cast = jnp.float32
     here = pl.multiple_of(q * N, N)
     sources = (
         packed.at[pl.ds(X_FORWARD + here, N)],
-        packed.at[pl.ds(Z_FORWARD, 8 * N)],
+        packed.at[pl.ds(Z_BOTH, 4 * N)],
         packed.at[pl.ds(Y_BOTH, N)],
         kernel,
-        packed.at[pl.ds(Z_BACK, 8 * N)],
         packed.at[pl.ds(X_BACK + here, N)],
     )
     loads = [
@@ -199,14 +201,15 @@
             wide += [mine * below, mine * above]
         done_x = left_dot(xf_ref[:, : 3 * N], jnp.concatenate(wide, axis=1))
         tall = jnp.concatenate(
-            [done_x[:, t * 256 : t * 256 + 256] for t in range(TILES)], axis=0
+            [done_x[:, t * 128 : t * 128 + 128] for t in range(2 * TILES)], axis=0
         )
-        done_z = right_dot(tall, zf_ref)
+        done_z = right_dot(tall, z_ref[...])
         for t in range(TILES):
-            part = done_z[t * N : t * N + N]
+            part = done_z[t * 2 * N : (t + 1) * 2 * N]
+            even, odd = woven(part[:N], part[N:])
             y = (c * TILES + t) * 2
-            work[pl.ds(pl.multiple_of(y * PITCH, 8), N), :] = part[:, :128]
-            work[pl.ds(pl.multiple_of(y * PITCH + PITCH, 8), N), :] = part[:, 128:]
+            work[pl.ds(pl.multiple_of(y * PITCH, 8), N), :] = even
+            work[pl.ds(pl.multiple_of(y * PITCH + PITCH, 8), N), :] = odd
 
     loads[2].wait()
     loads[3].wait()
@@ -216,13 +219,13 @@
         spots = [step * XSTEP + i for i in range(XSTEP)]
         value = jnp.concatenate([work[pl.ds(x, N, stride=PITCH), :] for x in spots], axis=1)
         value = left_dot(y_ref[:, : 3 * N], value)
-        weight = jnp.concatenate([k_ref[x] for x in spots], axis=1)
-        value = left_dot(y_ref[:, : 3 * N], value * weight)
+        plane = k_ref[:N]
+        level = [1.0 / (plane + k_ref[pl.ds(N + x, 1), :]) for x in spots]
+        value = left_dot(y_ref[:, : 3 * N], value * jnp.concatenate(level, axis=1))
         for i, x in enumerate(spots):
             work[pl.ds(x, N, stride=PITCH), :] = value[:, i * 128 : i * 128 + 128]
 
     loads[4].wait()
-    loads[5].wait()
 
     @pl.loop(0, LANES // CHUNK)
     def _(c):
@@ -231,9 +234,9 @@
             y = (c * TILES + t) * 2
             even = work[pl.ds(pl.multiple_of(y * PITCH, 8), N), :]
             odd = work[pl.ds(pl.multiple_of(y * PITCH + PITCH, 8), N), :]
-            parts.append(jnp.concatenate([even, odd], axis=1))
-        done_z = right_dot(jnp.concatenate(parts, axis=0), zb_ref)
-        wide = jnp.concatenate([done_z[t * N : t * N + N] for t in range(TILES)], axis=1)
+            parts += woven(even, odd)
+        done_z = right_dot(jnp.concatenate(parts, axis=0), z_ref[...])
+        wide = jnp.concatenate([done_z[t * N : t * N + N] for t in range(2 * TILES)], axis=1)
         pot = left_dot(xb_ref[:, : 3 * N], wide)
         for t in range(TILES):
             tile = c * TILES + t
@@ -327,13 +330,13 @@
             out_shape=[SENT] * 4,
             in_specs=[SMEM] + [VMEM] * 5 + [HBM] * 2,
             out_specs=[VMEM] * 4,
-            scratch_shapes=[pltpu.VMEM((N * PITCH, 128), jnp.float32)]
+            scratch_shapes=[pltpu.VMEM(((N + 1) * PITCH, 128), jnp.float32)]
             + [
-                pltpu.VMEM((rows, 4 * N), jnp.bfloat16) if rows else pltpu.VMEM((N, N, 2 * N), jnp.float32)
-                for rows in (N, 8 * N, N, 0, 8 * N, N)
+                pltpu.VMEM((rows, 4 * N), jnp.bfloat16) if rows else pltpu.VMEM((2 * N, 2 * N), jnp.float32)
+                for rows in (N, 4 * N, N, 0, N)
             ]
-            + [pltpu.SemaphoreType.DMA((6,))],
-            compiler_params=pltpu.CompilerParams(vmem_limit_bytes=50 * 1024 * 1024),
+            + [pltpu.SemaphoreType.DMA((5,))],
+            compiler_params=pltpu.CompilerParams(vmem_limit_bytes=49 * 1024 * 1024),
             cost_estimate=pl.CostEstimate(
                 flops=10_000_000_000, bytes_accessed=8_000_000, transcendentals=0
             ),

time: 139 us -> 138 us (level)
  Pallas kernels: 19 us -> 16.8 us
    pallas_call x2, Pallas kernels: 12 us -> 9.73 us  [on_device(): pl.pallas_call(functools.partial(solve, a), out_shape=[SENT] * 4, in_spec...]
where the time goes in v3:
time: 138 us
  waiting for transfers between devices  81.4 us (59%)
  starting transfers between devices  34.9 us (25%)
  Pallas kernels  16.8 us (12%)
  local copies, waits for them, and re-layouts  2.69 us (2%)
    all_to_all x1, waiting for transfers between devices, on_device(): held = lax.all_to_all(spread, 'band', 0, 0, tiled=True)  27.3 us
    ppermute x12, waiting for transfers between devices, across(): return lax.ppermute(value, 'pair', [(i, i ^ d) for i in range(PAIR)])  27.3 us
    all_to_all x1, waiting for transfers between devices, on_device(): seen = lax.all_to_all(routed, ('band', 'pair'), 0, 0, tiled=True)  26.8 us
    all_to_all x1, starting transfers between devices, on_device(): held = lax.all_to_all(spread, 'band', 0, 0, tiled=True)  15.1 us
    ppermute x12, starting transfers between devices, across(): return lax.ppermute(value, 'pair', [(i, i ^ d) for i in range(PAIR)])  10.8 us
    pallas_call x2, Pallas kernels, on_device(): pl.pallas_call(functools.partial(solve, a), out_shape=[SENT] * 4, in_spec...  9.73 us
    all_to_all x1, starting transfers between devices, on_device(): seen = lax.all_to_all(routed, ('band', 'pair'), 0, 0, tiled=True)  8.97 us
    pallas_call x1, Pallas kernels, on_device(): pl.pallas_call(route, out_shape=jax.ShapeDtypeStruct((SPOTS * PAIR, 4 * S...  3.25 us
  transfers between devices with their start and end apart: 14, of which 6 were waited for; matrix products, arithmetic and copies ran while one was open for 0% of the time, Pallas kernels for 5%

profile of v3, /device:TPU:1, one launch (start us, length us, event | category | flops | bytes accessed | tf_op | source)
XLA Modules:
  0.0 137.8 jit_solution(4824882654974071944)
XLA Ops:
  0.6 0.0 copy-start
  0.6 1.6 %copy-done = f32[8,16,4096]{2,1,0:T(8,128)S(1)} copy-done((f32[8,16,4096]{2,1,0:T(8,128)S(1)}, f32[8,16,4096]{2,1,0:T(8,128)}, u32[]{:S(2)}) %copy-start) | copy-done | bytes 2097176
  2.2 1.3 arrange.1
  3.5 15.1 %all-to-all-start = ((bf16[64,64,128]{2,1,0:T(8,128)(2,1)}), bf16[64,64,128]{2,1,0:T(8,128)(2,1)S(1)}, u32[]{:S(2)}, u32[]{:S(2)}) async-start(bf16[64,64,128]{2,1,0:T(8,128)(2,1)} %get-tuple-element.19), calls=%async_computation | async-start | bytes 2097152 | tf_op jit(solution)/shard_map/all_to_all | solution.py:309
  19.3 0.1 copy.7.table_ref
  19.4 27.3 %all-to-all-done.held_ref = bf16[64,64,128]{2,1,0:T(8,128)(2,1)S(1)} async-done(((bf16[64,64,128]{2,1,0:T(8,128)(2,1)}), bf16[64,64,128]{2,1,0:T(8,128)(2,1)S(1)}, u32[]{:S(2)}, u32[]{:S(2)}) %all-to-all-start) | async-done | bytes 1048608 | tf_op jit(solution)/shard_map/all_to_all | solution.py:309
  46.7 3.3 %route.1 = bf16[256,32,128]{2,1,0:T(8,128)(2,1)} custom-call(s32[8,2]{1,0:T(8,128)S(1)} %copy.7.table_ref, s32[1]{0:T(128)S(6)} %copy.8.offset_ref, bf16[64,64,128]{2,1,0:T(8,128)(2,1)S(1)} %all-to-all-done.held_ref), custom_call_target="tpu_custom_call" | custom-call | tf_op jit(solution)/shard_map/route/pallas_call | solution.py:310
  49.9 9.0 %all-to-all-start.1 = ((bf16[256,32,128]{2,1,0:T(8,128)(2,1)}), bf16[256,32,128]{2,1,0:T(8,128)(2,1)S(1)}, u32[]{:S(2)}, u32[]{:S(2)}) async-start(bf16[256,32,128]{2,1,0:T(8,128)(2,1)} %route.1), calls=%async_computation.1 | async-start | bytes 4194304 | tf_op jit(solution)/shard_map/all_to_all | solution.py:324
  58.9 2.2 %collective-permute-start = (bf16[2,16,4096]{2,1,0:T(8,128)(2,1)}, bf16[2,16,4096]{2,1,0:T(8,128)(2,1)S(1)}, u32[]{:S(2)}, u32[]{:S(2)}) collective-permute-start(bf16[2,16,4096]{2,1,0:T(8,128)(2,1)} %get-tuple-element.16), channel_id=1, source_target_pairs={{0,1},{1,0},{2,3},{3,2},{4,5},{5,4},{6,7},{7,6},{8,9},{9,8},{10,11... | collective-permute-start | bytes 786440 | tf_op jit(solution)/shard_map/ppermute | solution.py:298
  61.1 1.7 %collective-permute-start.2 = (bf16[2,16,4096]{2,1,0:T(8,128)(2,1)S(1)}, bf16[2,16,4096]{2,1,0:T(8,128)(2,1)S(1)}, u32[]{:S(2)}, u32[]{:S(2)}) collective-permute-start(bf16[2,16,4096]{2,1,0:T(8,128)(2,1)S(1)} %get-tuple-element.18), channel_id=1, source_target_pairs={{0,3},{1,2},{2,1},{3,0},{4,7},{5,6},{6,5},{7,4},{8,11},{9,10},{10,... | collective-permute-start | bytes 786440 | tf_op jit(solution)/shard_map/ppermute | solution.py:298
  62.9 11.0 %collective-permute-done.1.refs_2_ = bf16[2,16,4096]{2,1,0:T(8,128)(2,1)S(1)} collective-permute-done((bf16[2,16,4096]{2,1,0:T(8,128)(2,1)}, bf16[2,16,4096]{2,1,0:T(8,128)(2,1)S(1)}, u32[]{:S(2)}, u32[]{:S(2)}) %collective-permute-start.1) | collective-permute-done | bytes 262176 | tf_op jit(solution)/shard_map/ppermute | solution.py:298
  73.8 10.3 %collective-permute-done.2.refs_3_ = bf16[2,16,4096]{2,1,0:T(8,128)(2,1)S(1)} collective-permute-done((bf16[2,16,4096]{2,1,0:T(8,128)(2,1)S(1)}, bf16[2,16,4096]{2,1,0:T(8,128)(2,1)S(1)}, u32[]{:S(2)}, u32[]{:S(2)}) %collective-permute-start.2) | collective-permute-done | bytes 262176 | tf_op jit(solution)/shard_map/ppermute | solution.py:298
  84.1 26.8 %all-to-all-done.1.refs_4_ = bf16[256,32,128]{2,1,0:T(8,128)(2,1)S(1)} async-done(((bf16[256,32,128]{2,1,0:T(8,128)(2,1)}), bf16[256,32,128]{2,1,0:T(8,128)(2,1)S(1)}, u32[]{:S(2)}, u32[]{:S(2)}) %all-to-all-start.1) | async-done | bytes 2097184 | tf_op jit(solution)/shard_map/all_to_all | solution.py:324
  111.0 1.0 copy-done.2
  112.0 4.9 %solve.3 = (bf16[16,4096]{1,0:T(8,128)(2,1)S(1)}, bf16[16,4096]{1,0:T(8,128)(2,1)S(1)}, bf16[16,4096]{1,0:T(8,128)(2,1)S(1)}, bf16[16,4096]{1,0:T(8,128)(2,1)S(1)}) custom-call(s32[1]{0:T(128)} %bitcast.q_ref, bf16[2,16,4096]{2,1,0:T(8,128)(2,1)S(1)} %get-tuple-element.15.refs_0_, bf16[2,16,4096]{2,1,0:T(8,128)(2,1)S(1)} %collective-permute-done.refs_1_, ...), custom_call_target="tpu_custom_call" | custom-call | flops 10000000000 | bytes 8000000 | tf_op jit(solution)/shard_map/solve/pallas_call | solution.py:328
  116.9 0.7 collective-permute-start.6
  117.6 0.5 collective-permute-start.7
  118.1 1.2 collective-permute-start.8
  119.3 4.9 %solve.2 = (bf16[16,4096]{1,0:T(8,128)(2,1)S(1)}, bf16[16,4096]{1,0:T(8,128)(2,1)S(1)}, bf16[16,4096]{1,0:T(8,128)(2,1)S(1)}, bf16[16,4096]{1,0:T(8,128)(2,1)S(1)}) custom-call(s32[1]{0:T(128)} %bitcast.q_ref, bf16[2,16,4096]{2,1,0:T(8,128)(2,1)S(1)} %get-tuple-element.15.refs_0_, bf16[2,16,4096]{2,1,0:T(8,128)(2,1)S(1)} %collective-permute-done.refs_1_, ...), custom_call_target="tpu_custom_call" | custom-call | flops 10000000000 | bytes 8000000 | tf_op jit(solution)/shard_map/solve/pallas_call | solution.py:328
  124.2 0.2 collective-permute-start.3
  124.4 0.5 collective-permute-start.4
  124.9 1.5 %collective-permute-start.5 = (bf16[16,4096]{1,0:T(8,128)(2,1)S(1)}, bf16[16,4096]{1,0:T(8,128)(2,1)S(1)}, u32[]{:S(2)}, u32[]{:S(2)}) collective-permute-start(bf16[16,4096]{1,0:T(8,128)(2,1)S(1)} %get-tuple-element.23), channel_id=1, source_target_pairs={{0,3},{1,2},{2,1},{3,0},{4,7},{5,6},{6,5},{7,4},{8,11},{9,10},{10,... | collective-permute-start | bytes 393224 | tf_op jit(solution)/shard_map/ppermute | solution.py:298
  126.4 0.0 collective-permute-done.7.refs_6_
  126.4 0.0 collective-permute-done.8.refs_7_
  126.4 2.7 %collective-permute-done.4.refs_2_ = bf16[16,4096]{1,0:T(8,128)(2,1)S(1)} collective-permute-done((bf16[16,4096]{1,0:T(8,128)(2,1)S(1)}, bf16[16,4096]{1,0:T(8,128)(2,1)S(1)}, u32[]{:S(2)}, u32[]{:S(2)}) %collective-permute-start.4) | collective-permute-done | bytes 131104 | tf_op jit(solution)/shard_map/ppermute | solution.py:298
  129.1 3.3 %collective-permute-done.5.refs_3_ = bf16[16,4096]{1,0:T(8,128)(2,1)S(1)} collective-permute-done((bf16[16,4096]{1,0:T(8,128)(2,1)S(1)}, bf16[16,4096]{1,0:T(8,128)(2,1)S(1)}, u32[]{:S(2)}, u32[]{:S(2)}) %collective-permute-start.5) | collective-permute-done | bytes 131104 | tf_op jit(solution)/shard_map/ppermute | solution.py:298
  132.5 1.1 overlap.1
  133.5 0.3 collective-permute-start.11
  133.8 1.0 collective-permute-start.10
  134.8 0.9 collective-permute-start.9
  135.7 1.5 %widen.1 = f32[8,16,4096]{2,1,0:T(8,128)} custom-call(s32[1]{0:T(128)} %bitcast.q_ref, bf16[16,4096]{1,0:T(8,128)(2,1)S(1)} %get-tuple-element.20.refs_0_, bf16[16,4096]{1,0:T(8,128)(2,1)S(1)} %collective-permute-done.3.refs_1_, bf16[16,4096]{1,0:T(8,128)(2,1)S(1)} %collective-permute-done.4.refs_2_, bf16[16,4096]{1,0:T(8,128)(2,1)S(1)} %collective-permute-done.5.refs_3_, ...), custom_call_target="tpu_custom_call" | custom-call | bytes 8000000 | tf_op jit(solution)/shard_map/widen/pallas_call | solution.py:356
  137.2 0.6 add_add_fusion
  (14 shorter events, 0.0 us)
Async XLA Ops:
  0.6 1.6 %copy-start = (f32[8,16,4096]{2,1,0:T(8,128)S(1)}, f32[8,16,4096]{2,1,0:T(8,128)}, u32[]{:S(2)}) copy-start(f32[8,16,4096]{2,1,0:T(8,128)} %orb_ref.3) | copy-start | bytes 6291460
  2.2 17.1 %copy-start.4 = (s32[8,2]{0,1:T(2,128)S(1)}, s32[8,2]{0,1:T(2,128)}, u32[]{:S(2)}) copy-start(s32[8,2]{0,1:T(2,128)} %param.6) | copy-start | bytes 196
  3.5 43.2 %all-to-all-start = ((bf16[64,64,128]{2,1,0:T(8,128)(2,1)}), bf16[64,64,128]{2,1,0:T(8,128)(2,1)S(1)}, u32[]{:S(2)}, u32[]{:S(2)}) async-start(bf16[64,64,128]{2,1,0:T(8,128)(2,1)} %get-tuple-element.19), calls=%async_computation | async-start | bytes 2097152 | tf_op jit(solution)/shard_map/all_to_all | solution.py:309
  49.9 61.0 %copy-start.3 = (f32[128,128]{1,0:T(8,128)S(1)}, f32[128,128]{1,0:T(8,128)}, u32[]{:S(2)}) copy-start(f32[128,128]{1,0:T(8,128)} %constant.9.clone.refs_6_) | copy-start | bytes 196612
  49.9 61.0 %all-to-all-start.1 = ((bf16[256,32,128]{2,1,0:T(8,128)(2,1)}), bf16[256,32,128]{2,1,0:T(8,128)(2,1)S(1)}, u32[]{:S(2)}, u32[]{:S(2)}) async-start(bf16[256,32,128]{2,1,0:T(8,128)(2,1)} %route.1), calls=%async_computation.1 | async-start | bytes 4194304 | tf_op jit(solution)/shard_map/all_to_all | solution.py:324
  58.9 4.0 %collective-permute-start = (bf16[2,16,4096]{2,1,0:T(8,128)(2,1)}, bf16[2,16,4096]{2,1,0:T(8,128)(2,1)S(1)}, u32[]{:S(2)}, u32[]{:S(2)}) collective-permute-start(bf16[2,16,4096]{2,1,0:T(8,128)(2,1)} %get-tuple-element.16), channel_id=1, source_target_pairs={{0,1},{1,0},{2,3},{3,2},{4,5},{5,4},{6,7},{7,6},{8,9},{9,8},{10,11... | collective-permute-start | bytes 786440 | tf_op jit(solution)/shard_map/ppermute | solution.py:298
  61.1 12.7 %collective-permute-start.1 = (bf16[2,16,4096]{2,1,0:T(8,128)(2,1)}, bf16[2,16,4096]{2,1,0:T(8,128)(2,1)S(1)}, u32[]{:S(2)}, u32[]{:S(2)}) collective-permute-start(bf16[2,16,4096]{2,1,0:T(8,128)(2,1)} %get-tuple-element.17), channel_id=1, source_target_pairs={{0,2},{1,3},{2,0},{3,1},{4,6},{5,7},{6,4},{7,5},{8,10},{9,11},{10,... | collective-permute-start | bytes 786440 | tf_op jit(solution)/shard_map/ppermute | solution.py:298
  61.1 23.0 %collective-permute-start.2 = (bf16[2,16,4096]{2,1,0:T(8,128)(2,1)S(1)}, bf16[2,16,4096]{2,1,0:T(8,128)(2,1)S(1)}, u32[]{:S(2)}, u32[]{:S(2)}) collective-permute-start(bf16[2,16,4096]{2,1,0:T(8,128)(2,1)S(1)} %get-tuple-element.18), channel_id=1, source_target_pairs={{0,3},{1,2},{2,1},{3,0},{4,7},{5,6},{6,5},{7,4},{8,11},{9,10},{10,... | collective-permute-start | bytes 786440 | tf_op jit(solution)/shard_map/ppermute | solution.py:298
  111.0 1.0 copy-start.2
  116.9 8.0 %collective-permute-start.6 = (bf16[16,4096]{1,0:T(8,128)(2,1)S(1)}, bf16[16,4096]{1,0:T(8,128)(2,1)S(1)}, u32[]{:S(2)}, u32[]{:S(2)}) collective-permute-start(bf16[16,4096]{1,0:T(8,128)(2,1)S(1)} %get-tuple-element.25), channel_id=1, source_target_pairs={{0,1},{1,0},{2,3},{3,2},{4,5},{5,4},{6,7},{7,6},{8,9},{9,8},{10,11... | collective-permute-start | bytes 393224 | tf_op jit(solution)/shard_map/ppermute | solution.py:298
  117.6 8.8 %collective-permute-start.7 = (bf16[16,4096]{1,0:T(8,128)(2,1)S(1)}, bf16[16,4096]{1,0:T(8,128)(2,1)S(1)}, u32[]{:S(2)}, u32[]{:S(2)}) collective-permute-start(bf16[16,4096]{1,0:T(8,128)(2,1)S(1)} %get-tuple-element.26), channel_id=1, source_target_pairs={{0,2},{1,3},{2,0},{3,1},{4,6},{5,7},{6,4},{7,5},{8,10},{9,11},{10,... | collective-permute-start | bytes 393224 | tf_op jit(solution)/shard_map/ppermute | solution.py:298
  118.1 14.4 %copy-start.1 = (f32[8,16,4096]{2,1,0:T(8,128)S(1)}, f32[8,16,4096]{2,1,0:T(8,128)}, u32[]{:S(2)}) copy-start(f32[8,16,4096]{2,1,0:T(8,128)} %orb_ref.3) | copy-start | bytes 6291460
  118.1 8.3 %collective-permute-start.8 = (bf16[16,4096]{1,0:T(8,128)(2,1)S(1)}, bf16[16,4096]{1,0:T(8,128)(2,1)S(1)}, u32[]{:S(2)}, u32[]{:S(2)}) collective-permute-start(bf16[16,4096]{1,0:T(8,128)(2,1)S(1)} %get-tuple-element.27), channel_id=1, source_target_pairs={{0,3},{1,2},{2,1},{3,0},{4,7},{5,6},{6,5},{7,4},{8,11},{9,10},{10,... | collective-permute-start | bytes 393224 | tf_op jit(solution)/shard_map/ppermute | solution.py:298
  124.2 2.2 %collective-permute-start.3 = (bf16[16,4096]{1,0:T(8,128)(2,1)S(1)}, bf16[16,4096]{1,0:T(8,128)(2,1)S(1)}, u32[]{:S(2)}, u32[]{:S(2)}) collective-permute-start(bf16[16,4096]{1,0:T(8,128)(2,1)S(1)} %get-tuple-element.21), channel_id=1, source_target_pairs={{0,1},{1,0},{2,3},{3,2},{4,5},{5,4},{6,7},{7,6},{8,9},{9,8},{10,11... | collective-permute-start | bytes 393224 | tf_op jit(solution)/shard_map/ppermute | solution.py:298
  124.4 4.7 %collective-permute-start.4 = (bf16[16,4096]{1,0:T(8,128)(2,1)S(1)}, bf16[16,4096]{1,0:T(8,128)(2,1)S(1)}, u32[]{:S(2)}, u32[]{:S(2)}) collective-permute-start(bf16[16,4096]{1,0:T(8,128)(2,1)S(1)} %get-tuple-element.22), channel_id=1, source_target_pairs={{0,2},{1,3},{2,0},{3,1},{4,6},{5,7},{6,4},{7,5},{8,10},{9,11},{10,... | collective-permute-start | bytes 393224 | tf_op jit(solution)/shard_map/ppermute | solution.py:298
  124.9 7.5 %collective-permute-start.5 = (bf16[16,4096]{1,0:T(8,128)(2,1)S(1)}, bf16[16,4096]{1,0:T(8,128)(2,1)S(1)}, u32[]{:S(2)}, u32[]{:S(2)}) collective-permute-start(bf16[16,4096]{1,0:T(8,128)(2,1)S(1)} %get-tuple-element.23), channel_id=1, source_target_pairs={{0,3},{1,2},{2,1},{3,0},{4,7},{5,6},{6,5},{7,4},{8,11},{9,10},{10,... | collective-permute-start | bytes 393224 | tf_op jit(solution)/shard_map/ppermute | solution.py:298
  133.5 3.6 %collective-permute-start.11 = (f32[8,8]{1,0:T(8,128)S(1)}, f32[8,8]{1,0:T(8,128)S(1)}, u32[]{:S(2)}, u32[]{:S(2)}) collective-permute-start(f32[8,8]{1,0:T(8,128)S(1)} %overlap.1), channel_id=1, source_target_pairs={{0,3},{1,2},{2,1},{3,0},{4,7},{5,6},{6,5},{7,4},{8,11},{9,10},{10,... | collective-permute-start | bytes 776 | tf_op jit(solution)/shard_map/ppermute | solution.py:298
  133.8 3.4 %collective-permute-start.10 = (f32[8,8]{1,0:T(8,128)S(1)}, f32[8,8]{1,0:T(8,128)S(1)}, u32[]{:S(2)}, u32[]{:S(2)}) collective-permute-start(f32[8,8]{1,0:T(8,128)S(1)} %overlap.1), channel_id=1, source_target_pairs={{0,2},{1,3},{2,0},{3,1},{4,6},{5,7},{6,4},{7,5},{8,10},{9,11},{10,... | collective-permute-start | bytes 776 | tf_op jit(solution)/shard_map/ppermute | solution.py:298
  134.8 2.4 %collective-permute-start.9 = (f32[8,8]{1,0:T(8,128)S(1)}, f32[8,8]{1,0:T(8,128)S(1)}, u32[]{:S(2)}, u32[]{:S(2)}) collective-permute-start(f32[8,8]{1,0:T(8,128)S(1)} %overlap.1), channel_id=1, source_target_pairs={{0,1},{1,0},{2,3},{3,2},{4,5},{5,4},{6,7},{7,6},{8,9},{9,8},{10,11... | collective-permute-start | bytes 776 | tf_op jit(solution)/shard_map/ppermute | solution.py:298

commit v4 on v3

--- a/solution.py
+++ b/solution.py
@@ -27,7 +27,7 @@
 X_BACK = 256
 Z_BOTH = 512
 Y_BOTH = 768
-ROWS = 832
+ROWS = 4096
 VMEM_LIMIT = 48 * 1024 * 1024
 
 VMEM = pl.BlockSpec(memory_space=pltpu.VMEM)
@@ -336,13 +336,14 @@
                 for rows in (N, 4 * N, N, 0, N)
             ]
             + [pltpu.SemaphoreType.DMA((5,))],
-            compiler_params=pltpu.CompilerParams(vmem_limit_bytes=49 * 1024 * 1024),
+            compiler_params=pltpu.CompilerParams(vmem_limit_bytes=50 * 1024 * 1024),
             cost_estimate=pl.CostEstimate(
                 flops=10_000_000_000, bytes_accessed=8_000_000, transcendentals=0
             ),
             name="solve",
         )(q, *own, seen, *consts)
-        back += [sent[0]] + [across(sent[d], d) for d in range(1, PAIR)]
+        moved = {d: across(sent[d], d) for d in (3, 2, 1)}
+        back += [sent[0]] + [moved[d] for d in range(1, PAIR)]
     gram = pl.pallas_call(
         overlap,
         out_shape=jax.ShapeDtypeStruct((BLK, BLK), jnp.float32),

time: 138 us -> 138 us (level)
  no operation moved by 1% of the time
where the time goes in v4:
time: 138 us
  waiting for transfers between devices  81.4 us (59%)
  starting transfers between devices  34.9 us (25%)
  Pallas kernels  18 us (13%)
  local copies, waits for them, and re-layouts  1.68 us (1%)
    all_to_all x1, waiting for transfers between devices, on_device(): held = lax.all_to_all(spread, 'band', 0, 0, tiled=True)  27.3 us
    ppermute x12, waiting for transfers between devices, across(): return lax.ppermute(value, 'pair', [(i, i ^ d) for i in range(PAIR)])  27.3 us
    all_to_all x1, waiting for transfers between devices, on_device(): seen = lax.all_to_all(routed, ('band', 'pair'), 0, 0, tiled=True)  26.8 us
    all_to_all x1, starting transfers between devices, on_device(): held = lax.all_to_all(spread, 'band', 0, 0, tiled=True)  15.1 us
    pallas_call x2, Pallas kernels, on_device(): pl.pallas_call(functools.partial(solve, a), out_shape=[SENT] * 4, in_spec...  10.9 us
    ppermute x12, starting transfers between devices, across(): return lax.ppermute(value, 'pair', [(i, i ^ d) for i in range(PAIR)])  10.8 us
    all_to_all x1, starting transfers between devices, on_device(): seen = lax.all_to_all(routed, ('band', 'pair'), 0, 0, tiled=True)  8.97 us
    pallas_call x1, Pallas kernels, on_device(): pl.pallas_call(route, out_shape=jax.ShapeDtypeStruct((SPOTS * PAIR, 4 * S...  3.25 us
  transfers between devices with their start and end apart: 14, of which 6 were waited for; matrix products, arithmetic and copies ran while one was open for 0% of the time, Pallas kernels for 5%

profile of v4, /device:TPU:1, one launch (start us, length us, event | category | flops | bytes accessed | tf_op | source)
XLA Modules:
  0.0 137.9 jit_solution(318431419372363734)
XLA Ops:
  0.6 0.0 copy-start
  0.6 1.6 %copy-done = f32[8,16,4096]{2,1,0:T(8,128)S(1)} copy-done((f32[8,16,4096]{2,1,0:T(8,128)S(1)}, f32[8,16,4096]{2,1,0:T(8,128)}, u32[]{:S(2)}) %copy-start) | copy-done | bytes 2097176
  2.2 1.3 arrange.1
  3.5 15.1 %all-to-all-start = ((bf16[64,64,128]{2,1,0:T(8,128)(2,1)}), bf16[64,64,128]{2,1,0:T(8,128)(2,1)S(1)}, u32[]{:S(2)}, u32[]{:S(2)}) async-start(bf16[64,64,128]{2,1,0:T(8,128)(2,1)} %get-tuple-element.19), calls=%async_computation | async-start | bytes 2097152 | tf_op jit(solution)/shard_map/all_to_all | solution.py:309
  19.3 0.1 copy.7.table_ref
  19.4 27.3 %all-to-all-done.held_ref = bf16[64,64,128]{2,1,0:T(8,128)(2,1)S(1)} async-done(((bf16[64,64,128]{2,1,0:T(8,128)(2,1)}), bf16[64,64,128]{2,1,0:T(8,128)(2,1)S(1)}, u32[]{:S(2)}, u32[]{:S(2)}) %all-to-all-start) | async-done | bytes 1048608 | tf_op jit(solution)/shard_map/all_to_all | solution.py:309
  46.7 3.3 %route.1 = bf16[256,32,128]{2,1,0:T(8,128)(2,1)} custom-call(s32[8,2]{1,0:T(8,128)S(1)} %copy.7.table_ref, s32[1]{0:T(128)S(6)} %copy.8.offset_ref, bf16[64,64,128]{2,1,0:T(8,128)(2,1)S(1)} %all-to-all-done.held_ref), custom_call_target="tpu_custom_call" | custom-call | tf_op jit(solution)/shard_map/route/pallas_call | solution.py:310
  49.9 9.0 %all-to-all-start.1 = ((bf16[256,32,128]{2,1,0:T(8,128)(2,1)}), bf16[256,32,128]{2,1,0:T(8,128)(2,1)S(1)}, u32[]{:S(2)}, u32[]{:S(2)}) async-start(bf16[256,32,128]{2,1,0:T(8,128)(2,1)} %route.1), calls=%async_computation.1 | async-start | bytes 4194304 | tf_op jit(solution)/shard_map/all_to_all | solution.py:324
  58.9 2.2 %collective-permute-start = (bf16[2,16,4096]{2,1,0:T(8,128)(2,1)}, bf16[2,16,4096]{2,1,0:T(8,128)(2,1)S(1)}, u32[]{:S(2)}, u32[]{:S(2)}) collective-permute-start(bf16[2,16,4096]{2,1,0:T(8,128)(2,1)} %get-tuple-element.16), channel_id=1, source_target_pairs={{0,1},{1,0},{2,3},{3,2},{4,5},{5,4},{6,7},{7,6},{8,9},{9,8},{10,11... | collective-permute-start | bytes 786440 | tf_op jit(solution)/shard_map/ppermute | solution.py:298
  61.1 0.0 collective-permute-start.1
  61.2 1.7 %collective-permute-start.2 = (bf16[2,16,4096]{2,1,0:T(8,128)(2,1)S(1)}, bf16[2,16,4096]{2,1,0:T(8,128)(2,1)S(1)}, u32[]{:S(2)}, u32[]{:S(2)}) collective-permute-start(bf16[2,16,4096]{2,1,0:T(8,128)(2,1)S(1)} %get-tuple-element.18), channel_id=1, source_target_pairs={{0,3},{1,2},{2,1},{3,0},{4,7},{5,6},{6,5},{7,4},{8,11},{9,10},{10,... | collective-permute-start | bytes 786440 | tf_op jit(solution)/shard_map/ppermute | solution.py:298
  62.9 0.0 collective-permute-done.refs_1_
  62.9 11.0 %collective-permute-done.1.refs_2_ = bf16[2,16,4096]{2,1,0:T(8,128)(2,1)S(1)} collective-permute-done((bf16[2,16,4096]{2,1,0:T(8,128)(2,1)}, bf16[2,16,4096]{2,1,0:T(8,128)(2,1)S(1)}, u32[]{:S(2)}, u32[]{:S(2)}) %collective-permute-start.1) | collective-permute-done | bytes 262176 | tf_op jit(solution)/shard_map/ppermute | solution.py:298
  73.8 10.3 %collective-permute-done.2.refs_3_ = bf16[2,16,4096]{2,1,0:T(8,128)(2,1)S(1)} collective-permute-done((bf16[2,16,4096]{2,1,0:T(8,128)(2,1)S(1)}, bf16[2,16,4096]{2,1,0:T(8,128)(2,1)S(1)}, u32[]{:S(2)}, u32[]{:S(2)}) %collective-permute-start.2) | collective-permute-done | bytes 262176 | tf_op jit(solution)/shard_map/ppermute | solution.py:298
  84.1 26.8 %all-to-all-done.1.refs_4_ = bf16[256,32,128]{2,1,0:T(8,128)(2,1)S(1)} async-done(((bf16[256,32,128]{2,1,0:T(8,128)(2,1)}), bf16[256,32,128]{2,1,0:T(8,128)(2,1)S(1)}, u32[]{:S(2)}, u32[]{:S(2)}) %all-to-all-start.1) | async-done | bytes 2097184 | tf_op jit(solution)/shard_map/all_to_all | solution.py:324
  111.0 5.4 %solve.3 = (bf16[16,4096]{1,0:T(8,128)(2,1)S(1)}, bf16[16,4096]{1,0:T(8,128)(2,1)S(1)}, bf16[16,4096]{1,0:T(8,128)(2,1)S(1)}, bf16[16,4096]{1,0:T(8,128)(2,1)S(1)}) custom-call(s32[1]{0:T(128)} %bitcast.q_ref, bf16[2,16,4096]{2,1,0:T(8,128)(2,1)S(1)} %get-tuple-element.15.refs_0_, bf16[2,16,4096]{2,1,0:T(8,128)(2,1)S(1)} %collective-permute-done.refs_1_, ...), custom_call_target="tpu_custom_call" | custom-call | flops 10000000000 | bytes 8000000 | tf_op jit(solution)/shard_map/solve/pallas_call | solution.py:328
  116.4 0.7 collective-permute-start.6
  117.2 0.5 collective-permute-start.7
  117.7 1.2 collective-permute-start.8
  118.9 5.4 %solve.2 = (bf16[16,4096]{1,0:T(8,128)(2,1)S(1)}, bf16[16,4096]{1,0:T(8,128)(2,1)S(1)}, bf16[16,4096]{1,0:T(8,128)(2,1)S(1)}, bf16[16,4096]{1,0:T(8,128)(2,1)S(1)}) custom-call(s32[1]{0:T(128)} %bitcast.q_ref, bf16[2,16,4096]{2,1,0:T(8,128)(2,1)S(1)} %get-tuple-element.15.refs_0_, bf16[2,16,4096]{2,1,0:T(8,128)(2,1)S(1)} %collective-permute-done.refs_1_, ...), custom_call_target="tpu_custom_call" | custom-call | flops 10000000000 | bytes 8000000 | tf_op jit(solution)/shard_map/solve/pallas_call | solution.py:328
  124.3 0.2 collective-permute-start.3
  124.6 0.6 collective-permute-start.4
  125.2 0.0 collective-permute-done.6.refs_5_
  125.2 1.4 %collective-permute-start.5 = (bf16[16,4096]{1,0:T(8,128)(2,1)S(1)}, bf16[16,4096]{1,0:T(8,128)(2,1)S(1)}, u32[]{:S(2)}, u32[]{:S(2)}) collective-permute-start(bf16[16,4096]{1,0:T(8,128)(2,1)S(1)} %get-tuple-element.23), channel_id=1, source_target_pairs={{0,3},{1,2},{2,1},{3,0},{4,7},{5,6},{6,5},{7,4},{8,11},{9,10},{10,... | collective-permute-start | bytes 393224 | tf_op jit(solution)/shard_map/ppermute | solution.py:298
  126.6 2.7 %collective-permute-done.4.refs_2_ = bf16[16,4096]{1,0:T(8,128)(2,1)S(1)} collective-permute-done((bf16[16,4096]{1,0:T(8,128)(2,1)S(1)}, bf16[16,4096]{1,0:T(8,128)(2,1)S(1)}, u32[]{:S(2)}, u32[]{:S(2)}) %collective-permute-start.4) | collective-permute-done | bytes 131104 | tf_op jit(solution)/shard_map/ppermute | solution.py:298
  129.3 3.3 %collective-permute-done.5.refs_3_ = bf16[16,4096]{1,0:T(8,128)(2,1)S(1)} collective-permute-done((bf16[16,4096]{1,0:T(8,128)(2,1)S(1)}, bf16[16,4096]{1,0:T(8,128)(2,1)S(1)}, u32[]{:S(2)}, u32[]{:S(2)}) %collective-permute-start.5) | collective-permute-done | bytes 131104 | tf_op jit(solution)/shard_map/ppermute | solution.py:298
  132.6 1.1 overlap.1
  133.7 0.5 collective-permute-start.11
  134.2 0.7 collective-permute-start.10
  134.9 0.9 collective-permute-start.9
  135.8 1.5 %widen.1 = f32[8,16,4096]{2,1,0:T(8,128)} custom-call(s32[1]{0:T(128)} %bitcast.q_ref, bf16[16,4096]{1,0:T(8,128)(2,1)S(1)} %get-tuple-element.20.refs_0_, bf16[16,4096]{1,0:T(8,128)(2,1)S(1)} %collective-permute-done.3.refs_1_, bf16[16,4096]{1,0:T(8,128)(2,1)S(1)} %collective-permute-done.4.refs_2_, bf16[16,4096]{1,0:T(8,128)(2,1)S(1)} %collective-permute-done.5.refs_3_, ...), custom_call_target="tpu_custom_call" | custom-call | bytes 8000000 | tf_op jit(solution)/shard_map/widen/pallas_call | solution.py:357
  137.3 0.6 add_add_fusion
  (12 shorter events, 0.0 us)
Async XLA Ops:
  0.6 1.6 %copy-start = (f32[8,16,4096]{2,1,0:T(8,128)S(1)}, f32[8,16,4096]{2,1,0:T(8,128)}, u32[]{:S(2)}) copy-start(f32[8,16,4096]{2,1,0:T(8,128)} %orb_ref.3) | copy-start | bytes 6291460
  2.2 17.1 %copy-start.3 = (s32[8,2]{0,1:T(2,128)S(1)}, s32[8,2]{0,1:T(2,128)}, u32[]{:S(2)}) copy-start(s32[8,2]{0,1:T(2,128)} %param.6) | copy-start | bytes 196
  3.5 43.2 %all-to-all-start = ((bf16[64,64,128]{2,1,0:T(8,128)(2,1)}), bf16[64,64,128]{2,1,0:T(8,128)(2,1)S(1)}, u32[]{:S(2)}, u32[]{:S(2)}) async-start(bf16[64,64,128]{2,1,0:T(8,128)(2,1)} %get-tuple-element.19), calls=%async_computation | async-start | bytes 2097152 | tf_op jit(solution)/shard_map/all_to_all | solution.py:309
  49.9 61.0 %copy-start.2 = (f32[128,128]{1,0:T(8,128)S(1)}, f32[128,128]{1,0:T(8,128)}, u32[]{:S(2)}) copy-start(f32[128,128]{1,0:T(8,128)} %constant.9.clone.refs_6_) | copy-start | bytes 196612
  49.9 61.0 %all-to-all-start.1 = ((bf16[256,32,128]{2,1,0:T(8,128)(2,1)}), bf16[256,32,128]{2,1,0:T(8,128)(2,1)S(1)}, u32[]{:S(2)}, u32[]{:S(2)}) async-start(bf16[256,32,128]{2,1,0:T(8,128)(2,1)} %route.1), calls=%async_computation.1 | async-start | bytes 4194304 | tf_op jit(solution)/shard_map/all_to_all | solution.py:324
  58.9 4.0 %collective-permute-start = (bf16[2,16,4096]{2,1,0:T(8,128)(2,1)}, bf16[2,16,4096]{2,1,0:T(8,128)(2,1)S(1)}, u32[]{:S(2)}, u32[]{:S(2)}) collective-permute-start(bf16[2,16,4096]{2,1,0:T(8,128)(2,1)} %get-tuple-element.16), channel_id=1, source_target_pairs={{0,1},{1,0},{2,3},{3,2},{4,5},{5,4},{6,7},{7,6},{8,9},{9,8},{10,11... | collective-permute-start | bytes 786440 | tf_op jit(solution)/shard_map/ppermute | solution.py:298
  61.1 12.7 %collective-permute-start.1 = (bf16[2,16,4096]{2,1,0:T(8,128)(2,1)}, bf16[2,16,4096]{2,1,0:T(8,128)(2,1)S(1)}, u32[]{:S(2)}, u32[]{:S(2)}) collective-permute-start(bf16[2,16,4096]{2,1,0:T(8,128)(2,1)} %get-tuple-element.17), channel_id=1, source_target_pairs={{0,2},{1,3},{2,0},{3,1},{4,6},{5,7},{6,4},{7,5},{8,10},{9,11},{10,... | collective-permute-start | bytes 786440 | tf_op jit(solution)/shard_map/ppermute | solution.py:298
  61.2 23.0 %collective-permute-start.2 = (bf16[2,16,4096]{2,1,0:T(8,128)(2,1)S(1)}, bf16[2,16,4096]{2,1,0:T(8,128)(2,1)S(1)}, u32[]{:S(2)}, u32[]{:S(2)}) collective-permute-start(bf16[2,16,4096]{2,1,0:T(8,128)(2,1)S(1)} %get-tuple-element.18), channel_id=1, source_target_pairs={{0,3},{1,2},{2,1},{3,0},{4,7},{5,6},{6,5},{7,4},{8,11},{9,10},{10,... | collective-permute-start | bytes 786440 | tf_op jit(solution)/shard_map/ppermute | solution.py:298
  116.4 8.7 %collective-permute-start.6 = (bf16[16,4096]{1,0:T(8,128)(2,1)S(1)}, bf16[16,4096]{1,0:T(8,128)(2,1)S(1)}, u32[]{:S(2)}, u32[]{:S(2)}) collective-permute-start(bf16[16,4096]{1,0:T(8,128)(2,1)S(1)} %get-tuple-element.25), channel_id=1, source_target_pairs={{0,1},{1,0},{2,3},{3,2},{4,5},{5,4},{6,7},{7,6},{8,9},{9,8},{10,11... | collective-permute-start | bytes 393224 | tf_op jit(solution)/shard_map/ppermute | solution.py:298
  117.2 9.4 %collective-permute-start.7 = (bf16[16,4096]{1,0:T(8,128)(2,1)S(1)}, bf16[16,4096]{1,0:T(8,128)(2,1)S(1)}, u32[]{:S(2)}, u32[]{:S(2)}) collective-permute-start(bf16[16,4096]{1,0:T(8,128)(2,1)S(1)} %get-tuple-element.26), channel_id=1, source_target_pairs={{0,2},{1,3},{2,0},{3,1},{4,6},{5,7},{6,4},{7,5},{8,10},{9,11},{10,... | collective-permute-start | bytes 393224 | tf_op jit(solution)/shard_map/ppermute | solution.py:298
  117.7 14.9 %copy-start.1 = (f32[8,16,4096]{2,1,0:T(8,128)S(1)}, f32[8,16,4096]{2,1,0:T(8,128)}, u32[]{:S(2)}) copy-start(f32[8,16,4096]{2,1,0:T(8,128)} %orb_ref.3) | copy-start | bytes 6291460
  117.7 8.9 %collective-permute-start.8 = (bf16[16,4096]{1,0:T(8,128)(2,1)S(1)}, bf16[16,4096]{1,0:T(8,128)(2,1)S(1)}, u32[]{:S(2)}, u32[]{:S(2)}) collective-permute-start(bf16[16,4096]{1,0:T(8,128)(2,1)S(1)} %get-tuple-element.27), channel_id=1, source_target_pairs={{0,3},{1,2},{2,1},{3,0},{4,7},{5,6},{6,5},{7,4},{8,11},{9,10},{10,... | collective-permute-start | bytes 393224 | tf_op jit(solution)/shard_map/ppermute | solution.py:298
  124.3 2.2 %collective-permute-start.3 = (bf16[16,4096]{1,0:T(8,128)(2,1)S(1)}, bf16[16,4096]{1,0:T(8,128)(2,1)S(1)}, u32[]{:S(2)}, u32[]{:S(2)}) collective-permute-start(bf16[16,4096]{1,0:T(8,128)(2,1)S(1)} %get-tuple-element.21), channel_id=1, source_target_pairs={{0,1},{1,0},{2,3},{3,2},{4,5},{5,4},{6,7},{7,6},{8,9},{9,8},{10,11... | collective-permute-start | bytes 393224 | tf_op jit(solution)/shard_map/ppermute | solution.py:298
  124.6 4.7 %collective-permute-start.4 = (bf16[16,4096]{1,0:T(8,128)(2,1)S(1)}, bf16[16,4096]{1,0:T(8,128)(2,1)S(1)}, u32[]{:S(2)}, u32[]{:S(2)}) collective-permute-start(bf16[16,4096]{1,0:T(8,128)(2,1)S(1)} %get-tuple-element.22), channel_id=1, source_target_pairs={{0,2},{1,3},{2,0},{3,1},{4,6},{5,7},{6,4},{7,5},{8,10},{9,11},{10,... | collective-permute-start | bytes 393224 | tf_op jit(solution)/shard_map/ppermute | solution.py:298
  125.2 7.4 %collective-permute-start.5 = (bf16[16,4096]{1,0:T(8,128)(2,1)S(1)}, bf16[16,4096]{1,0:T(8,128)(2,1)S(1)}, u32[]{:S(2)}, u32[]{:S(2)}) collective-permute-start(bf16[16,4096]{1,0:T(8,128)(2,1)S(1)} %get-tuple-element.23), channel_id=1, source_target_pairs={{0,3},{1,2},{2,1},{3,0},{4,7},{5,6},{6,5},{7,4},{8,11},{9,10},{10,... | collective-permute-start | bytes 393224 | tf_op jit(solution)/shard_map/ppermute | solution.py:298
  133.7 3.6 %collective-permute-start.11 = (f32[8,8]{1,0:T(8,128)S(1)}, f32[8,8]{1,0:T(8,128)S(1)}, u32[]{:S(2)}, u32[]{:S(2)}) collective-permute-start(f32[8,8]{1,0:T(8,128)S(1)} %overlap.1), channel_id=1, source_target_pairs={{0,3},{1,2},{2,1},{3,0},{4,7},{5,6},{6,5},{7,4},{8,11},{9,10},{10,... | collective-permute-start | bytes 776 | tf_op jit(solution)/shard_map/ppermute | solution.py:298
  134.2 3.1 %collective-permute-start.10 = (f32[8,8]{1,0:T(8,128)S(1)}, f32[8,8]{1,0:T(8,128)S(1)}, u32[]{:S(2)}, u32[]{:S(2)}) collective-permute-start(f32[8,8]{1,0:T(8,128)S(1)} %overlap.1), channel_id=1, source_target_pairs={{0,2},{1,3},{2,0},{3,1},{4,6},{5,7},{6,4},{7,5},{8,10},{9,11},{10,... | collective-permute-start | bytes 776 | tf_op jit(solution)/shard_map/ppermute | solution.py:298
  134.9 2.4 %collective-permute-start.9 = (f32[8,8]{1,0:T(8,128)S(1)}, f32[8,8]{1,0:T(8,128)S(1)}, u32[]{:S(2)}, u32[]{:S(2)}) collective-permute-start(f32[8,8]{1,0:T(8,128)S(1)} %overlap.1), channel_id=1, source_target_pairs={{0,1},{1,0},{2,3},{3,2},{4,5},{5,4},{6,7},{7,6},{8,9},{9,8},{10,11... | collective-permute-start | bytes 776 | tf_op jit(solution)/shard_map/ppermute | solution.py:298
